TPU v7x, 256 devices: a whole 4x4x8 slice. The times are simulated.
256 devices in a mesh: round: 32 (over x, z_lo, core), head: 4 (over y), rep: 2 (over z_hi).
Axes of the slice: x: 4, y: 4, z: 8 (z_hi: 2, z_lo: 4; z = z_hi * 4 + z_lo), core: 2. Of those that a mesh axis runs over, the one named last changes fastest.
Arguments:
- query_rows: bfloat16 [8192, 8192], P(('rep', 'round'), 'head'), parts along dimension 0, may hold values from -12 to 12
- table_key_rows: bfloat16 [8192, 1024], P(('rep', 'round'), 'head'), parts along dimension 0, may hold values from -4 to 4
- table_value_rows: bfloat16 [8192, 1024], P(('rep', 'round'), 'head'), parts along dimension 0, may hold values from -6 to 6
- out_grad: bfloat16 [8192, 8192], P(('rep', 'round'), 'head'), parts along dimension 0, may hold values from -96 to 96
- round_lengths: int32 [32], P('rep'), parts along dimension 0, may hold values from 1 to 768, 4096 in all
- assignment: int32 [128], P('rep'), parts along dimension 0, may hold values from 0 to 63, as said below
Outputs:
- query_grad: bfloat16 [8192, 8192], P(('rep', 'round'), 'head'), parts along dimension 0
- key_gradient: bfloat16 [8192, 1024], P(('rep', 'round'), 'head'), parts along dimension 0
- value_gradient: bfloat16 [8192, 1024], P(('rep', 'round'), 'head'), parts along dimension 0
There are 2 independent parts, one for each index of `rep`. A program takes and returns all parts, laid end to end along the dimension named above; each array names one. Nothing has to cross between parts.
Inputs may be any that keep to these rules, and one draw needn't show every extreme that they name: `round_lengths`: the 16 lengths sum to 4096; the longest is exactly 768. `assignment`: each block number appears once; entries 2i and 2i + 1 sum to 63.
All inputs are finite; a program needn't handle non-finite values.
Results may differ from a plain program's by a relative error of at most 0.005.
Values may be sent and summed in bfloat16 or wider, within the bound.
A program may use at most 128 MiB of HBM per device.

v0:
```python
import math

import jax
import jax.numpy as jnp
from jax import lax
from jax.sharding import PartitionSpec as P

HEAD_SIZE = 128
RWIN = 8


far_below = -1e30


def seq_positions(assignment, first_row, piece_rows, half_rows):
    row_index = first_row + jnp.arange(piece_rows, dtype=jnp.int32)
    block_index = row_index // half_rows
    block_slots = jnp.arange(assignment.shape[0], dtype=jnp.int32)
    picked = jnp.sum(
        jnp.where(block_index[:, None] == block_slots[None, :], assignment[None, :], 0), axis=1
    )
    return picked * half_rows + row_index % half_rows


def round_ids(positions, round_ends):
    return jnp.sum((positions[:, None] >= round_ends[None, :]).astype(jnp.int32), axis=1)


def regroup(matrix, kv_heads, query_group_width):
    local_rows = matrix.shape[0]
    shaped = matrix.reshape(local_rows, kv_heads, query_group_width, HEAD_SIZE).transpose(
        1, 2, 0, 3
    )
    return shaped.reshape(kv_heads, query_group_width * local_rows, HEAD_SIZE)


def per_device(query_rows, table_key_rows, table_value_rows, out_grad, round_lengths, assignment):
    rows_here = query_rows.shape[0]
    half_rows = rows_here // 2
    kv_width = table_key_rows.shape[1]
    kv_heads = kv_width // HEAD_SIZE
    query_group_width = query_rows.shape[1] // kv_width
    score_scale = HEAD_SIZE ** (-0.5)
    round_ends = jnp.cumsum(round_lengths)[:-1]
    query_pos = seq_positions(assignment, lax.axis_index("round") * rows_here, rows_here, half_rows)
    row_pos = jnp.tile(query_pos, query_group_width)
    row_round = jnp.tile(round_ids(query_pos, round_ends), query_group_width)
    q_grouped = regroup(query_rows, kv_heads, query_group_width)
    g_grouped = regroup(out_grad, kv_heads, query_group_width)
    rows_all = query_group_width * rows_here

    def visible_of(key_block, key_first):
        key_pos = seq_positions(assignment, key_first, key_block.shape[0], half_rows)
        key_round = round_ids(key_pos, round_ends)
        return (key_pos[None, :] <= row_pos[:, None]) & (
            key_round[None, :] > row_round[:, None] - RWIN
        )

    def scores_of(key_block, value_block):
        block_rows = key_block.shape[0]
        heads_of_key = key_block.reshape(block_rows, kv_heads, HEAD_SIZE)
        heads_of_value = value_block.reshape(block_rows, kv_heads, HEAD_SIZE)
        scores = (
            jnp.einsum("hrd,nhd->hrn", q_grouped, heads_of_key, preferred_element_type=jnp.float32)
            * score_scale
        )
        dprobs = jnp.einsum(
            "hrd,nhd->hrn", g_grouped, heads_of_value, preferred_element_type=jnp.float32
        )
        return (scores, dprobs, heads_of_key)

    def split_blocks(gathered, start_row):
        key_piece, value_piece = gathered
        piece_rows = key_piece.shape[0]
        block_rows = math.gcd(piece_rows, 512)
        block_count = piece_rows // block_rows
        offsets = start_row + block_rows * jnp.arange(block_count, dtype=jnp.int32)
        key_blocks = key_piece.reshape(block_count, block_rows, kv_width)
        value_blocks = value_piece.reshape(block_count, block_rows, kv_width)
        return (key_blocks, value_blocks, offsets, block_rows)

    start_stats = (
        jnp.full((kv_heads, rows_all), far_below, jnp.float32),
        jnp.zeros((kv_heads, rows_all), jnp.float32),
        jnp.zeros((kv_heads, rows_all), jnp.float32),
    )
    zero_query = jnp.zeros((kv_heads, rows_all, HEAD_SIZE), jnp.float32)
    key_all, value_all = (
        lax.all_gather(table_key_rows, "round", axis=0, tiled=True),
        lax.all_gather(table_value_rows, "round", axis=0, tiled=True),
    )
    fold_state = start_stats
    key_blocks, value_blocks, offsets, block_rows = split_blocks((key_all, value_all), 0)

    def stats_step(stats_now, scan_item):
        key_block, value_block, key_first = scan_item
        visible = visible_of(key_block, key_first)

        def stats_work(stats_in):
            row_top, row_total, weighted = stats_in
            scores, dprobs, unused_heads = scores_of(key_block, value_block)
            scores = jnp.where(visible[None], scores, far_below)
            new_top = jnp.maximum(row_top, jnp.max(scores, axis=2))
            rescale = jnp.exp(row_top - new_top)
            prob_block = jnp.where(visible[None], jnp.exp(scores - new_top[:, :, None]), 0.0)
            return (
                new_top,
                row_total * rescale + jnp.sum(prob_block, axis=2),
                weighted * rescale + jnp.sum(prob_block * dprobs, axis=2),
            )

        return (lax.cond(jnp.any(visible), stats_work, lambda stats_in: stats_in, stats_now), None)

    fold_state, unused_out = lax.scan(stats_step, fold_state, (key_blocks, value_blocks, offsets))
    row_top, row_total, weighted = fold_state
    log_total = row_top + jnp.log(row_total)
    row_delta = weighted / row_total
    query_acc = zero_query
    grad_query_acc = query_acc
    key_blocks, value_blocks, offsets, block_rows = split_blocks((key_all, value_all), 0)
    zero_part = jnp.zeros((block_rows, kv_width), jnp.float32)

    def grad_step(query_now, scan_item):
        key_block, value_block, key_first = scan_item
        visible = visible_of(key_block, key_first)

        def grad_work(query_in):
            scores, dprobs, heads_of_key = scores_of(key_block, value_block)
            prob_block = jnp.where(visible[None], jnp.exp(scores - log_total[:, :, None]), 0.0)
            dscores = prob_block * (dprobs - row_delta[:, :, None])
            dscores_b = dscores.astype(jnp.bfloat16)
            prob_b = prob_block.astype(jnp.bfloat16)
            value_portion = jnp.einsum(
                "hrn,hrd->nhd", prob_b, g_grouped, preferred_element_type=jnp.float32
            ).reshape(block_rows, kv_width)
            key_portion = (
                jnp.einsum(
                    "hrn,hrd->nhd", dscores_b, q_grouped, preferred_element_type=jnp.float32
                ).reshape(block_rows, kv_width)
                * score_scale
            )
            query_in = (
                query_in
                + jnp.einsum(
                    "hrn,nhd->hrd", dscores_b, heads_of_key, preferred_element_type=jnp.float32
                )
                * score_scale
            )
            return (query_in, key_portion, value_portion)

        def grad_skip(query_in):
            return (query_in, zero_part, zero_part)

        query_now, key_portion, value_portion = lax.cond(
            jnp.any(visible), grad_work, grad_skip, query_now
        )
        return (query_now, (key_portion, value_portion))

    grad_query_acc, (key_parts, value_parts) = lax.scan(
        grad_step, grad_query_acc, (key_blocks, value_blocks, offsets)
    )
    query_acc, key_parts, value_parts = (
        grad_query_acc,
        key_parts.reshape(-1, kv_width),
        value_parts.reshape(-1, kv_width),
    )
    key_all_grad = key_parts
    value_all_grad = value_parts
    query_acc, key_all_grad, value_all_grad = (query_acc, key_all_grad, value_all_grad)
    key_gradient, value_gradient = (
        lax.psum_scatter(key_all_grad, "round", scatter_dimension=0, tiled=True),
        lax.psum_scatter(value_all_grad, "round", scatter_dimension=0, tiled=True),
    )
    query_grad = query_acc.reshape(kv_heads, query_group_width, rows_here, HEAD_SIZE).transpose(
        2, 0, 1, 3
    )
    query_grad = query_grad.reshape(rows_here, kv_heads * query_group_width * HEAD_SIZE).astype(
        jnp.bfloat16
    )
    return (query_grad, key_gradient.astype(jnp.bfloat16), value_gradient.astype(jnp.bfloat16))


def solution(mesh):
    return jax.shard_map(
        per_device,
        mesh=mesh,
        in_specs=(
            P(("rep", "round"), "head"),
            P(("rep", "round"), "head"),
            P(("rep", "round"), "head"),
            P(("rep", "round"), "head"),
            P("rep"),
            P("rep"),
        ),
        out_specs=(
            P(("rep", "round"), "head"),
            P(("rep", "round"), "head"),
            P(("rep", "round"), "head"),
        ),
        check_vma=False,
    )
```

profile of v0, /device:TPU:1, one launch (start us, length us, event | category | flops | bytes accessed | tf_op | source)
XLA Modules:
  0.0 632.5 jit_solution(15063456143074865196)
XLA Ops:
  15.2 59.1 %all-gather.3.cloned.1.call-done = bf16[4096,256]{1,0:T(8,128)(2,1)} async-done(((bf16[128,256]{1,0:T(8,128)(2,1)}), bf16[4096,256]{1,0:T(8,128)(2,1)}) %all-gather.3.cloned.1.call-update) | async-done | bytes 2097168 | tf_op jit(solution)/shard_map/all_gather | solution.py:89
  74.3 3.9 copy.79
  78.2 57.0 %all-gather.5.cloned.1.call-done = bf16[4096,256]{1,0:T(8,128)(2,1)} async-done(((bf16[128,256]{1,0:T(8,128)(2,1)}), bf16[4096,256]{1,0:T(8,128)(2,1)}) %all-gather.5.cloned.1.call-update) | async-done | bytes 2097168 | tf_op jit(solution)/shard_map/all_gather | solution.py:90
  135.2 3.9 copy.77
  139.2 73.8 %while.37 = (s32[]{:T(128)}, f32[2,1024]{1,0:T(2,128)S(1)}, f32[2,1024]{1,0:T(2,128)S(1)}, f32[2,1024]{1,0:T(2,128)S(1)}, s32[8]{0:T(128)S(1)}, /*index=5*/s32[6...) while((s32[]{:T(128)}, f32[2,1024]{1,0:T(2,128)S(1)}, ...), condition=%wide.region_12.13_spmd.clone, body=%wide.region_3.12_spmd.clone.sunk | while | flops 553790080 | bytes 17486440 | solution.py:114
  143.4 5.0 conditional.6
  152.6 5.0 conditional.6
  161.8 5.0 conditional.6
  171.0 5.0 conditional.6
  180.3 5.0 conditional.6
  189.5 5.0 conditional.6
  198.7 5.0 conditional.6
  208.0 5.0 conditional.6
  213.1 112.7 %while.38 = (s32[]{:T(128)}, f32[2,1024,128]{2,1,0:T(8,128)S(1)}, f32[8,512,256]{2,1,0:T(8,128)}, f32[8,512,256]{2,1,0:T(8,128)}, s32[8]{0:T(128)S(1)}, /*index=...) while((s32[]{:T(128)}, f32[2,1024,128]{2,1,0:T(8,128)S(1)}, ...), condition=%wide.region_19.20_spmd.clone, body=%wide.region_13.19_spmd.clone.sunk | while | flops 1355551360 | bytes 31781976 | solution.py:159
  217.1 8.7 %conditional.7 = (f32[2,1024,128]{2,1,0:T(8,128)S(1)}, f32[1,512,256]{1,2,0:T(8,128)S(1)}, f32[1,512,256]{1,2,0:T(8,128)S(1)}) conditional(s32[]{:T(128)} %convert_element_type.79, f32[2,1024,128]{2,1,0:T(8,128)S(1)} %get-tuple-element.1039, (pred[1024,512]{0,1:T(8,128)(4,1)S(1)}, bf16[8,512,256]{1,2,0:T(8,128)(2,1)}, s32[]{:T(128)}, ...), branch_computations={%region_17.17_spmd, %region_18.18_spmd} | conditional | flops 1353318400 | bytes 27025436 | solution.py:154
  221.2 2.5 fusion.11
  231.1 8.7 %conditional.7 = (f32[2,1024,128]{2,1,0:T(8,128)S(1)}, f32[1,512,256]{1,2,0:T(8,128)S(1)}, f32[1,512,256]{1,2,0:T(8,128)S(1)}) conditional(s32[]{:T(128)} %convert_element_type.79, f32[2,1024,128]{2,1,0:T(8,128)S(1)} %get-tuple-element.1039, (pred[1024,512]{0,1:T(8,128)(4,1)S(1)}, bf16[8,512,256]{1,2,0:T(8,128)(2,1)}, s32[]{:T(128)}, ...), branch_computations={%region_17.17_spmd, %region_18.18_spmd} | conditional | flops 1353318400 | bytes 27025436 | solution.py:154
  235.3 2.5 fusion.11
  245.2 8.7 %conditional.7 = (f32[2,1024,128]{2,1,0:T(8,128)S(1)}, f32[1,512,256]{1,2,0:T(8,128)S(1)}, f32[1,512,256]{1,2,0:T(8,128)S(1)}) conditional(s32[]{:T(128)} %convert_element_type.79, f32[2,1024,128]{2,1,0:T(8,128)S(1)} %get-tuple-element.1039, (pred[1024,512]{0,1:T(8,128)(4,1)S(1)}, bf16[8,512,256]{1,2,0:T(8,128)(2,1)}, s32[]{:T(128)}, ...), branch_computations={%region_17.17_spmd, %region_18.18_spmd} | conditional | flops 1353318400 | bytes 27025436 | solution.py:154
  249.3 2.5 fusion.11
  259.3 8.7 %conditional.7 = (f32[2,1024,128]{2,1,0:T(8,128)S(1)}, f32[1,512,256]{1,2,0:T(8,128)S(1)}, f32[1,512,256]{1,2,0:T(8,128)S(1)}) conditional(s32[]{:T(128)} %convert_element_type.79, f32[2,1024,128]{2,1,0:T(8,128)S(1)} %get-tuple-element.1039, (pred[1024,512]{0,1:T(8,128)(4,1)S(1)}, bf16[8,512,256]{1,2,0:T(8,128)(2,1)}, s32[]{:T(128)}, ...), branch_computations={%region_17.17_spmd, %region_18.18_spmd} | conditional | flops 1353318400 | bytes 27025436 | solution.py:154
  263.4 2.5 fusion.11
  273.4 8.7 %conditional.7 = (f32[2,1024,128]{2,1,0:T(8,128)S(1)}, f32[1,512,256]{1,2,0:T(8,128)S(1)}, f32[1,512,256]{1,2,0:T(8,128)S(1)}) conditional(s32[]{:T(128)} %convert_element_type.79, f32[2,1024,128]{2,1,0:T(8,128)S(1)} %get-tuple-element.1039, (pred[1024,512]{0,1:T(8,128)(4,1)S(1)}, bf16[8,512,256]{1,2,0:T(8,128)(2,1)}, s32[]{:T(128)}, ...), branch_computations={%region_17.17_spmd, %region_18.18_spmd} | conditional | flops 1353318400 | bytes 27025436 | solution.py:154
  277.5 2.5 fusion.11
  287.5 8.7 %conditional.7 = (f32[2,1024,128]{2,1,0:T(8,128)S(1)}, f32[1,512,256]{1,2,0:T(8,128)S(1)}, f32[1,512,256]{1,2,0:T(8,128)S(1)}) conditional(s32[]{:T(128)} %convert_element_type.79, f32[2,1024,128]{2,1,0:T(8,128)S(1)} %get-tuple-element.1039, (pred[1024,512]{0,1:T(8,128)(4,1)S(1)}, bf16[8,512,256]{1,2,0:T(8,128)(2,1)}, s32[]{:T(128)}, ...), branch_computations={%region_17.17_spmd, %region_18.18_spmd} | conditional | flops 1353318400 | bytes 27025436 | solution.py:154
  291.6 2.5 fusion.11
  301.6 8.7 %conditional.7 = (f32[2,1024,128]{2,1,0:T(8,128)S(1)}, f32[1,512,256]{1,2,0:T(8,128)S(1)}, f32[1,512,256]{1,2,0:T(8,128)S(1)}) conditional(s32[]{:T(128)} %convert_element_type.79, f32[2,1024,128]{2,1,0:T(8,128)S(1)} %get-tuple-element.1039, (pred[1024,512]{0,1:T(8,128)(4,1)S(1)}, bf16[8,512,256]{1,2,0:T(8,128)(2,1)}, s32[]{:T(128)}, ...), branch_computations={%region_17.17_spmd, %region_18.18_spmd} | conditional | flops 1353318400 | bytes 27025436 | solution.py:154
  305.7 2.5 fusion.11
  315.7 8.7 %conditional.7 = (f32[2,1024,128]{2,1,0:T(8,128)S(1)}, f32[1,512,256]{1,2,0:T(8,128)S(1)}, f32[1,512,256]{1,2,0:T(8,128)S(1)}) conditional(s32[]{:T(128)} %convert_element_type.79, f32[2,1024,128]{2,1,0:T(8,128)S(1)} %get-tuple-element.1039, (pred[1024,512]{0,1:T(8,128)(4,1)S(1)}, bf16[8,512,256]{1,2,0:T(8,128)(2,1)}, s32[]{:T(128)}, ...), branch_computations={%region_17.17_spmd, %region_18.18_spmd} | conditional | flops 1353318400 | bytes 27025436 | solution.py:154
  319.8 2.5 fusion.11
  327.8 144.9 %reduce-scatter.5.cloned.1.call-done = f32[128,256]{1,0:T(8,128)} async-done(((f32[4096,256]{1,0:T(8,128)}), f32[128,256]{1,0:T(8,128)}) %reduce-scatter.5.cloned.1.call-update) | async-done | bytes 131088 | tf_op jit(solution)/shard_map/reduce_scatter | solution.py:172
  474.3 150.2 %reduce-scatter.3.cloned.1.call-done = f32[128,256]{1,0:T(8,128)} async-done(((f32[4096,256]{1,0:T(8,128)}), f32[128,256]{1,0:T(8,128)}) %reduce-scatter.3.cloned.1.call-update) | async-done | bytes 131088 | tf_op jit(solution)/shard_map/reduce_scatter | solution.py:171
  (296 shorter events, 168.0 us)
Async XLA Ops:
  7.2 4.6 copy-start
  7.2 67.1 %all-gather.3.cloned.1.call-start = ((), (), s32[]{:S(2)}) async-start(), calls=%async_computation.2 | async-start | bytes 2162688 | tf_op jit(solution)/shard_map/all_gather | solution.py:89
  7.9 127.3 %all-gather.5.cloned.1.call-start = ((), (), s32[]{:S(2)}) async-start(), calls=%async_computation.3 | async-start | bytes 2162688 | tf_op jit(solution)/shard_map/all_gather | solution.py:90
  8.7 464.1 %reduce-scatter.5.cloned.1.call-start = ((), (), s32[]{:S(2)}) async-start(), calls=%async_computation.5 | async-start | bytes 4325376 | tf_op jit(solution)/shard_map/reduce_scatter | solution.py:172
  9.5 5.5 copy-start.1
  325.8 298.6 %reduce-scatter.3.cloned.1.call-start = ((), (), s32[]{:S(2)}) async-start(), calls=%async_computation.4 | async-start | bytes 4325376 | tf_op jit(solution)/shard_map/reduce_scatter | solution.py:171
Sparse Core Ops, SparseCore 0:
  9.9 64.3 all-gather.2
  76.1 59.0 all-gather.4
  326.0 146.6 reduce-scatter.4
  475.1 149.2 reduce-scatter.2
where the time goes:
time: 638 us; the launch traced here: 632 us
  waiting for transfers between devices  413 us (65%)
  matrix products  82.7 us (13%)
  other arithmetic  57 us (9%)
  local copies, waits for them, and re-layouts  54.1 us (8%)
  between operations  13.9 us (2%)
  loops' own time  11.5 us (2%)
    reduce_scatter x1, waiting for transfers between devices, per_device(): lax.psum_scatter(key_all_grad, 'round', scatter_dimension=0, tiled=True)  150 us
    reduce_scatter x1, waiting for transfers between devices, per_device(): lax.psum_scatter(value_all_grad, 'round', scatter_dimension=0, tiled=True)  145 us
    all_gather x1, waiting for transfers between devices, per_device(): lax.all_gather(table_key_rows, 'round', axis=0, tiled=True)  59.1 us
    all_gather x1, waiting for transfers between devices, per_device(): lax.all_gather(table_value_rows, 'round', axis=0, tiled=True)  57 us
    dot_general x16, matrix products, scores_of(): jnp.einsum('hrd,nhd->hrn', g_grouped, heads_of_value, preferred_element_t...  33.7 us
    dynamic_slice x32, local copies, waits for them, and re-layouts, per_device(): lax.scan(stats_step, fold_state, (key_blocks, value_blocks, offsets))  27.2 us
    dot_general x8, matrix products, grad_work(): jnp.einsum('hrn,hrd->nhd', prob_b, g_grouped, preferred_element_type=jnp....  18.1 us
    dot_general x16, matrix products, scores_of(): jnp.einsum('hrd,nhd->hrn', q_grouped, heads_of_key, preferred_element_typ...  14.6 us
  transfers between devices with their start and end apart: 4, of which 4 were waited for; matrix products, arithmetic and copies ran while one was open for 2% of the time, Pallas kernels for 0%

commit v1 on v0

v1 whole, which is shorter than its diff:
```python
import functools
import math

import jax
import jax.numpy as jnp
from jax import lax
from jax.experimental import pallas as pl
from jax.experimental.pallas import tpu as pltpu
from jax.sharding import PartitionSpec as P

HEAD_SIZE = 128
RWIN = 8
HALF = 64
RING = 4
LINE = 4
GROUP_HEADS = 8
COLS = GROUP_HEADS * HALF
SCALE = HEAD_SIZE**-0.5
SCALE2 = SCALE * math.log2(math.e)
FAR = -1e30
MESH = pl.DeviceIdType.MESH
F32 = jnp.float32
BF16 = jnp.bfloat16


def mul_nt(a, b):
    return lax.dot_general(a, b, (((1,), (1,)), ((), ())), preferred_element_type=F32)


def mul_nn(a, b):
    return lax.dot_general(a, b, (((1,), (0,)), ((), ())), preferred_element_type=F32)


def mul_tn(a, b):
    return lax.dot_general(a, b, (((0,), (0,)), ((), ())), preferred_element_type=F32)


def kernel(
    q_ref, k_ref, v_ref, g_ref, len_ref, asg_ref,
    dq_ref, dk_ref, dv_ref,
    kv, qin, gin, qcat, gcat, stats, start, dqacc, part, dextra, dqout, fin,
    s1r, s1l, r1l, r1r, s2r, s2l, r2l, r2r, s3, r3,
    local_sem, send_sem, recv_sem,
):
    blocks = asg_ref.shape[0]
    me = lax.axis_index("round")
    core, chip = lax.rem(me, 2), lax.div(me, 2)
    z, x = lax.rem(chip, LINE), lax.div(chip, LINE)
    sib = 1 - core

    def device(xx, zz, cc):
        return {"round": (xx * LINE + zz) * 2 + cc}

    def xat(k):
        return lax.rem(x + k, RING)

    def zat(k):
        return lax.rem(z + k, LINE)

    used = [0]

    def remote(src, dst, target):
        i = used[0]
        used[0] = i + 1
        return pltpu.make_async_remote_copy(
            src_ref=src, dst_ref=dst, send_sem=send_sem.at[i], recv_sem=recv_sem.at[i],
            device_id=target, device_id_type=MESH,
        )

    right, left = device(xat(1), z, core), device(xat(RING - 1), z, core)
    brother = device(x, z, sib)
    along_z = [None] + [device(x, zat(k), core) for k in range(1, LINE)]

    barrier = pltpu.get_barrier_semaphore()
    peers = [brother, right, left] + along_z[1:]
    for peer in peers:
        pl.semaphore_signal(barrier, inc=1, device_id=peer, device_id_type=MESH)
    pl.semaphore_wait(barrier, len(peers))

    def lanes(index, width):
        return pl.ds(pl.multiple_of(index * width, width), width)

    mine = z * RING + x
    own_rows, sib_rows = lanes(core, 128), lanes(sib, 128)
    wide = GROUP_HEADS * HEAD_SIZE
    swaps = [
        remote(k_ref.at[:, lanes(sib, 128)], kv.at[mine, 0, own_rows, :], brother),
        remote(v_ref.at[:, lanes(sib, 128)], kv.at[mine, 1, own_rows, :], brother),
        remote(q_ref.at[:, lanes(sib, wide)], qin.at[1], brother),
        remote(g_ref.at[:, lanes(sib, wide)], gin.at[1], brother),
    ]
    for swap in swaps:
        swap.start()
    own = [
        pltpu.make_async_copy(k_ref.at[:, lanes(core, 128)], kv.at[mine, 0, own_rows, :], local_sem.at[0]),
        pltpu.make_async_copy(v_ref.at[:, lanes(core, 128)], kv.at[mine, 1, own_rows, :], local_sem.at[1]),
        pltpu.make_async_copy(q_ref.at[:, lanes(core, wide)], qin.at[0], local_sem.at[2]),
        pltpu.make_async_copy(g_ref.at[:, lanes(core, wide)], gin.at[0], local_sem.at[3]),
    ]
    for copy in own:
        copy.start()
    own[0].wait()
    own[1].wait()
    swaps[0].wait_recv()
    swaps[1].wait_recv()

    def slot(xx, zz):
        return zz * RING + xx

    zsend = [None] + [remote(kv.at[mine], kv.at[mine], along_z[k]) for k in range(1, LINE)]
    xright = [remote(kv.at[slot(x, zat(k))], kv.at[slot(x, zat(k))], right) for k in range(LINE)]
    xleft = [remote(kv.at[slot(x, zat(k))], kv.at[slot(x, zat(k))], left) for k in range(LINE)]
    fright = [
        remote(kv.at[slot(xat(RING - 1), zat(k)), 0], kv.at[slot(xat(RING - 1), zat(k)), 0], right)
        for k in range(LINE)
    ]
    fleft = [
        remote(kv.at[slot(xat(1), zat(k)), 1], kv.at[slot(xat(1), zat(k)), 1], left)
        for k in range(LINE)
    ]
    order = [0, LINE - 1, 1, 2]
    xright[0].start()
    xleft[0].start()
    for k in (1, LINE - 1, 2):
        zsend[k].start()

    def relay(k):
        xright[k].wait_recv()
        fright[k].start()
        xleft[k].wait_recv()
        fleft[k].start()

    for n, k in enumerate(order):
        if n > 0:
            zsend[LINE - k].wait_recv()
            xright[k].start()
            xleft[k].start()
            relay(order[n - 1])
    relay(order[-1])
    for k in order:
        fright[k].wait_recv()
        fleft[k].wait_recv()
    own[2].wait()
    own[3].wait()
    swaps[2].wait_recv()
    swaps[3].wait_recv()

    pairs = [2 * chip + core, 2 * chip + sib]

    def pair_small(pair):
        first, second = asg_ref[2 * pair], asg_ref[2 * pair + 1]
        return jnp.minimum(first, second), (first > second).astype(jnp.int32)

    ends, total = [], 0
    for j in range(15):
        total = total + len_ref[j]
        ends.append(total)
    lane_row = lax.rem(lax.broadcasted_iota(jnp.int32, (8, COLS), 1), HALF)
    sub_row = lax.broadcasted_iota(jnp.int32, (8, COLS), 0)
    for p in range(2):
        small, flag = pair_small(pairs[p])
        for side in range(2):
            turned = flag == 1 - side
            for h in range(GROUP_HEADS):
                to = (p, slice(h * HALF, (h + 1) * HALF), slice(side * 128, side * 128 + 128))
                cols = slice(h * 128, h * 128 + 128)
                qcat[to] = jnp.where(turned, qin[p, HALF:, cols], qin[p, :HALF, cols])
                gcat[to] = jnp.where(turned, gin[p, HALF:, cols], gin[p, :HALF, cols])
            base = (small if side == 0 else blocks - 1 - small) * HALF
            first = jnp.zeros((8, COLS), jnp.int32)
            for j in range(15 - RWIN + 1):
                first = jnp.where(base + lane_row >= ends[j + RWIN - 1], ends[j], first)
            start[p, side] = first - sub_row
            stats[0, p, side] = jnp.full((8, COLS), FAR, F32)
            stats[1, p, side] = jnp.zeros((8, COLS), F32)
            stats[2, p, side] = jnp.zeros((8, COLS), F32)
        dqacc[p] = jnp.zeros((COLS, 256), F32)

    eight = 8 * lax.broadcasted_iota(jnp.int32, (8, 8, COLS), 0)
    never = 1 << 20

    def load_pairs(first_slot, slots):
        small_k, large_k, small_v, large_v, firsts, flags = [], [], [], [], [], []
        for t in range(2 * slots):
            at = first_slot + t // 2
            pair = (lax.rem(at, RING) * LINE + lax.div(at, RING)) * 2 + t % 2
            small, flag = pair_small(pair)
            row = (t % 2) * 128
            turned = flag == 1
            for n, small_n, large_n in ((0, small_k, large_k), (1, small_v, large_v)):
                lo, hi = kv[at, n, row : row + HALF, :], kv[at, n, row + HALF : row + 128, :]
                small_n.append(jnp.where(turned, hi, lo))
                large_n.append(jnp.where(turned, lo, hi))
            firsts.append(small)
            flags.append(flag)
        return small_k, large_k, small_v, large_v, firsts, flags

    def halves(sel, small, large):
        zero = jnp.zeros_like(small)
        return jnp.concatenate(
            [jnp.where(sel, small, zero), jnp.where(sel, zero, large)], axis=1
        )

    def units(loaded, p):
        small_k, large_k, small_v, large_v, firsts, unused_flags = loaded
        mine_small, unused_flag = pair_small(pairs[p])
        tile_a, tile_b = [], []
        sels = []
        for j in firsts:
            sel = j < mine_small
            sels.append(sel)
            tile_a.append((None, start[p, 1] - j * HALF))
            begin = jnp.where(sel, start[p, 0] - j * HALF, start[p, 1] - (blocks - 1 - j) * HALF)
            tile_b.append((sel, jnp.where(j == mine_small, never, begin)))
        keys_a = jnp.concatenate(small_k, axis=0)
        values_a = jnp.concatenate(small_v, axis=0)
        keys_b = jnp.concatenate([halves(*b) for b in zip(sels, small_k, large_k)], axis=0)
        values_b = jnp.concatenate([halves(*b) for b in zip(sels, small_v, large_v)], axis=0)
        return (keys_a, values_a, tile_a, 1), (keys_b, values_b, tile_b, 0)

    def side_of(sel, ref_at):
        if sel is None:
            return ref_at(1)
        return jnp.where(sel, ref_at(0), ref_at(1))

    def products(p, keys, values, first_side):
        width = slice(128, 256) if first_side == 1 else slice(0, 256)
        return mul_nt(keys, qcat[p, :, width]), mul_nt(values, gcat[p, :, width])

    def stats_unit(p, sel, mask, scores, dprobs):
        scores = jnp.where(mask, scores * SCALE2, FAR)
        top = side_of(sel, lambda side: stats[0, p, side])
        new_top = jnp.maximum(top, jnp.max(scores, axis=0))
        rescale = jnp.exp2(top - new_top)
        probs = jnp.exp2(scores - new_top[None])
        total = side_of(sel, lambda side: stats[1, p, side]) * rescale + jnp.sum(probs, axis=0)
        weighted = side_of(sel, lambda side: stats[2, p, side]) * rescale + jnp.sum(
            probs * dprobs, axis=0
        )
        for n, new in enumerate((new_top, total, weighted)):
            if sel is None:
                stats[n, p, 1] = new
            else:
                old = stats[n, p, 1]
                stats[n, p, 0] = jnp.where(sel, new, stats[n, p, 0])
                stats[n, p, 1] = jnp.where(sel, old, new)

    def stats_pass(first_slot, slots):
        loaded = load_pairs(first_slot, slots)
        for p in range(2):
            for keys, values, tiles, first_side in units(loaded, p):
                scores, dprobs = products(p, keys, values, first_side)
                for t, (sel, begin) in enumerate(tiles):
                    rows = slice(t * HALF, (t + 1) * HALF)
                    stats_unit(
                        p, sel, eight >= begin[None],
                        scores[rows].reshape(8, 8, COLS), dprobs[rows].reshape(8, 8, COLS),
                    )

    def grad_unit(p, sel, mask, scores, dprobs):
        scores = jnp.where(mask, scores * SCALE2, FAR)
        log_total = side_of(sel, lambda side: stats[0, p, side])
        delta = side_of(sel, lambda side: stats[1, p, side])
        probs = jnp.exp2(scores - log_total[None])
        dscores = probs * (dprobs - delta[None])
        return (
            probs.reshape(HALF, COLS).astype(BF16),
            dscores.reshape(HALF, COLS).astype(BF16),
        )

    def grad_tile(p, keys, values, tiles, first_side):
        width = slice(128, 256) if first_side == 1 else slice(0, 256)
        scores, dprobs = products(p, keys, values, first_side)
        probs_b, dscores_b = [], []
        for t, (sel, mask) in enumerate(tiles):
            rows = slice(t * HALF, (t + 1) * HALF)
            one, two = grad_unit(
                p, sel, mask,
                scores[rows].reshape(8, 8, COLS), dprobs[rows].reshape(8, 8, COLS),
            )
            probs_b.append(one)
            dscores_b.append(two)
        probs_b = jnp.concatenate(probs_b, axis=0)
        dscores_b = jnp.concatenate(dscores_b, axis=0)
        dqacc[p, :, width] += mul_tn(dscores_b, keys)
        return mul_nn(dscores_b, qcat[p, :, width]), mul_nn(probs_b, gcat[p, :, width])

    def grad_pass(first_slot, slots):
        loaded = load_pairs(first_slot, slots)
        flags = loaded[-1]
        small = [0.0, 0.0]
        large = [0.0, 0.0]
        for p in range(2):
            (ka, va, ta, unused_a), (kb, vb, tb, unused_b) = units(loaded, p)
            ta = [(sel, eight >= begin[None]) for sel, begin in ta]
            masks_b = [(sel, eight >= begin[None]) for sel, begin in tb]
            grads_a = grad_tile(p, ka, va, ta, 1)
            grads_b = grad_tile(p, kb, vb, masks_b, 0)
            for n in range(2):
                small[n] = small[n] + grads_a[n]
                zero = jnp.zeros((HALF, 128), F32)
                add_small, add_large = [], []
                for t, (sel, unused_mask) in enumerate(tb):
                    rows = slice(t * HALF, (t + 1) * HALF)
                    add_small.append(jnp.where(sel, grads_b[n][rows, :128], zero))
                    add_large.append(jnp.where(sel, zero, grads_b[n][rows, 128:]))
                small[n] = small[n] + jnp.concatenate(add_small, axis=0)
                large[n] = large[n] + jnp.concatenate(add_large, axis=0)
        for n in range(2):
            for t, flag in enumerate(flags):
                rows = slice(t * HALF, (t + 1) * HALF)
                at, row = first_slot + t // 2, (t % 2) * 128
                turned = flag == 1
                lo, hi = small[n][rows], large[n][rows]
                part[at, n, row : row + HALF, :] = jnp.where(turned, hi, lo)
                part[at, n, row + HALF : row + 128, :] = jnp.where(turned, lo, hi)

    tri = lax.broadcasted_iota(jnp.int32, (8, 8, COLS), 1) + eight <= lax.rem(
        lax.broadcasted_iota(jnp.int32, (8, 8, COLS), 2), HALF
    )

    def own_tile(p):
        rows = own_rows if p == 0 else sib_rows
        small, flag = pair_small(pairs[p])
        turned = flag == 1
        zero = jnp.zeros((HALF, 128), BF16)

        def stack(n):
            pair = kv[mine, n, rows, :]
            lo, hi = pair[:HALF], pair[HALF:]
            return jnp.concatenate(
                [
                    jnp.concatenate([jnp.where(turned, hi, lo), zero], axis=1),
                    jnp.concatenate([zero, jnp.where(turned, lo, hi)], axis=1),
                ],
                axis=0,
            )

        masks = []
        for side in range(2):
            base = (small if side == 0 else blocks - 1 - small) * HALF
            masks.append(tri & (eight >= (start[p, side] - base)[None]))
        return stack(0), stack(1), masks, flag

    def side_const(side):
        return side == 0

    for p in range(2):
        keys, values, masks, unused_flag = own_tile(p)
        scores, dprobs = products(p, keys, values, 0)
        for side in range(2):
            rows = slice(side * HALF, (side + 1) * HALF)
            s = jnp.where(masks[side], scores[rows].reshape(8, 8, COLS) * SCALE2, FAR)
            top = jnp.max(s, axis=0)
            probs = jnp.exp2(s - top[None])
            stats[0, p, side] = top
            stats[1, p, side] = jnp.sum(probs, axis=0)
            stats[2, p, side] = jnp.sum(probs * dprobs[rows].reshape(8, 8, COLS), axis=0)

    tile_slots = 2

    @pl.loop(0, RING * LINE // tile_slots)
    def _(n):
        stats_pass(n * tile_slots, tile_slots)

    for p in range(2):
        for side in range(2):
            top = stats[0, p, side]
            best = jnp.max(top, axis=0, keepdims=True)
            weight = jnp.exp2(top - best)
            total = jnp.sum(stats[1, p, side] * weight, axis=0, keepdims=True)
            weighted = jnp.sum(stats[2, p, side] * weight, axis=0, keepdims=True)
            stats[0, p, side] = jnp.broadcast_to(best + jnp.log2(total), (8, COLS))
            stats[1, p, side] = jnp.broadcast_to(weighted / total, (8, COLS))

    @pl.loop(0, RING * LINE // tile_slots)
    def _(n):
        grad_pass(n * tile_slots, tile_slots)

    for p in range(2):
        keys, values, masks, flag = own_tile(p)
        tiles = [(True, masks[0]), (False, masks[1])]
        grads = grad_tile(p, keys, values, tiles, 0)
        rows = own_rows if p == 0 else sib_rows
        for n in range(2):
            lo, hi = grads[n][:HALF, :128], grads[n][HALF:, 128:]
            turned = flag == 1
            dextra[...] = jnp.concatenate(
                [jnp.where(turned, hi, lo), jnp.where(turned, lo, hi)], axis=0
            )
            part[mine, n, rows, :] += dextra[...]

    for p in range(2):
        unused_small, flag = pair_small(pairs[p])
        turned = flag == 1
        for h in range(GROUP_HEADS):
            both = dqacc[p, h * HALF : (h + 1) * HALF, :] * SCALE
            lo, hi = both[:, :128], both[:, 128:]
            dqout[p, :HALF, h * 128 : h * 128 + 128] = jnp.where(turned, hi, lo).astype(BF16)
            dqout[p, HALF:, h * 128 : h * 128 + 128] = jnp.where(turned, lo, hi).astype(BF16)
    dq_out = remote(dqout.at[1], dq_ref.at[:, lanes(core, wide)], brother)
    dq_out.start()
    dq_own = pltpu.make_async_copy(dqout.at[0], dq_ref.at[:, lanes(core, wide)], local_sem.at[4])
    dq_own.start()

    back = [LINE - 1, 2, 1, 0]
    far_x = [xat(2), xat(1), xat(RING - 1), x]
    c1r = [remote(s1r.at[k], r1l.at[k], right) for k in range(LINE)]
    c1l = [remote(s1l.at[k], r1r.at[k], left) for k in range(LINE)]
    c2r = [remote(s2r.at[k], r2l.at[k], right) for k in range(LINE)]
    c2l = [remote(s2l.at[k], r2r.at[k], left) for k in range(LINE)]
    c3 = [None] + [remote(s3.at[k], r3.at[k], along_z[k]) for k in range(1, LINE)]
    for k in back:
        s1r[k] = part[slot(far_x[0], zat(k)), 0].astype(BF16)
        c1r[k].start()
        s1l[k] = part[slot(far_x[0], zat(k)), 1].astype(BF16)
        c1l[k].start()
    for k in back:
        to_right, to_left = slot(far_x[1], zat(k)), slot(far_x[2], zat(k))
        s2r[k, 1] = part[to_right, 1].astype(BF16)
        s2l[k, 0] = part[to_left, 0].astype(BF16)
        c1r[k].wait_recv()
        s2r[k, 0] = (part[to_right, 0] + r1l[k].astype(F32)).astype(BF16)
        c2r[k].start()
        c1l[k].wait_recv()
        s2l[k, 1] = (part[to_left, 1] + r1r[k].astype(F32)).astype(BF16)
        c2l[k].start()
    for k in back:
        c2r[k].wait_recv()
        c2l[k].wait_recv()
        whole = part[slot(x, zat(k))] + r2l[k].astype(F32) + r2r[k].astype(F32)
        if k > 0:
            s3[k] = whole.astype(BF16)
            c3[k].start()
        else:
            part[mine] = whole
    for k in range(1, LINE):
        c3[k].wait_recv()
    for n, factor in ((0, SCALE), (1, 1.0)):
        whole = part[mine, n]
        for k in range(1, LINE):
            whole = whole + r3[k, n].astype(F32)
        fin[n] = (whole * factor).astype(BF16)
    outs = [
        remote(fin.at[0, sib_rows, :], dk_ref.at[:, lanes(core, 128)], brother),
        remote(fin.at[1, sib_rows, :], dv_ref.at[:, lanes(core, 128)], brother),
    ]
    for out in outs:
        out.start()
    keep = [
        pltpu.make_async_copy(fin.at[0, own_rows, :], dk_ref.at[:, lanes(core, 128)], local_sem.at[5]),
        pltpu.make_async_copy(fin.at[1, own_rows, :], dv_ref.at[:, lanes(core, 128)], local_sem.at[6]),
    ]
    for copy in keep:
        copy.start()
    dq_own.wait()
    for copy in keep:
        copy.wait()
    dq_out.wait_recv()
    for out in outs:
        out.wait_recv()
    for copy in (
        swaps + zsend[1:] + xright + xleft + fright + fleft + [dq_out] + c1r + c1l + c2r + c2l + c3[1:] + outs
    ):
        copy.wait_send()


COPIES = 4 + 3 + 4 * LINE + 1 + 4 * LINE + 3 + 2


def per_device(q, k, v, g, lengths, assignment):
    slots = RING * LINE
    anywhere = pl.BlockSpec(memory_space=pl.ANY)
    vmem = pl.BlockSpec(memory_space=pltpu.VMEM)
    smem = pl.BlockSpec(memory_space=pltpu.SMEM)
    half = (LINE, 256, 128)
    full = (LINE, 2, 256, 128)
    return pl.pallas_call(
        kernel,
        out_shape=(
            jax.ShapeDtypeStruct(q.shape, BF16),
            jax.ShapeDtypeStruct(k.shape, BF16),
            jax.ShapeDtypeStruct(v.shape, BF16),
        ),
        in_specs=[anywhere] * 4 + [smem] * 2,
        out_specs=(vmem, vmem, vmem),
        scratch_shapes=[
            pltpu.VMEM((slots, 2, 256, 128), BF16),
            pltpu.VMEM((2, 128, 1024), BF16),
            pltpu.VMEM((2, 128, 1024), BF16),
            pltpu.VMEM((2, COLS, 256), BF16),
            pltpu.VMEM((2, COLS, 256), BF16),
            pltpu.VMEM((3, 2, 2, 8, COLS), F32),
            pltpu.VMEM((2, 2, 8, COLS), jnp.int32),
            pltpu.VMEM((2, COLS, 256), F32),
            pltpu.VMEM((slots, 2, 256, 128), F32),
            pltpu.VMEM((128, 128), F32),
            pltpu.VMEM((2, 128, 1024), BF16),
            pltpu.VMEM((2, 256, 128), BF16),
            pltpu.VMEM(half, BF16),
            pltpu.VMEM(half, BF16),
            pltpu.VMEM(half, BF16),
            pltpu.VMEM(half, BF16),
            pltpu.VMEM(full, BF16),
            pltpu.VMEM(full, BF16),
            pltpu.VMEM(full, BF16),
            pltpu.VMEM(full, BF16),
            pltpu.VMEM(full, BF16),
            pltpu.VMEM(full, BF16),
            pltpu.SemaphoreType.DMA((7,)),
            pltpu.SemaphoreType.DMA((COPIES,)),
            pltpu.SemaphoreType.DMA((COPIES,)),
        ],
        compiler_params=pltpu.CompilerParams(
            collective_id=0, has_side_effects=True, vmem_limit_bytes=50 * 1024 * 1024
        ),
    )(q, k, v, g, lengths, assignment)


def solution(mesh):
    return jax.shard_map(
        per_device,
        mesh=mesh,
        in_specs=(
            P(("rep", "round"), "head"),
            P(("rep", "round"), "head"),
            P(("rep", "round"), "head"),
            P(("rep", "round"), "head"),
            P("rep"),
            P("rep"),
        ),
        out_specs=(
            P(("rep", "round"), "head"),
            P(("rep", "round"), "head"),
            P(("rep", "round"), "head"),
        ),
        check_vma=False,
    )
```

time: 638 us -> 93.6 us (0.15)
  waiting for transfers between devices: 413 us -> 0 us
  Pallas kernels: 0 us -> 85.6 us
  matrix products: 82.7 us -> 0 us
  other arithmetic: 57 us -> 0 us
  local copies, waits for them, and re-layouts: 54.1 us -> 7.12 us
  between operations: 13.9 us -> 0.65 us
  loops' own time: 11.5 us -> 0 us
    reduce_scatter x2 -> x0, waiting for transfers between devices: 295 us -> none  [the longest x1 150 us: per_device(): lax.psum_scatter(key_all_grad, 'round', scatter_dimension=0, tiled=True)]
    all_gather x2 -> x0, waiting for transfers between devices: 116 us -> none  [the longest x1 59.1 us: per_device(): lax.all_gather(table_key_rows, 'round', axis=0, tiled=True)]
    pallas_call x0 -> x1, Pallas kernels: none -> 85.6 us  [per_device(): pl.pallas_call(kernel, out_shape=(jax.ShapeDtypeStruct(q.shape, BF16), ja...]
    dot_general x56 -> x0, matrix products: 82.7 us -> none  [the longest x16 33.7 us: scores_of(): jnp.einsum('hrd,nhd->hrn', g_grouped, heads_of_value, preferred_element_t...]
    dynamic_slice x32 -> x0, local copies, waits for them, and re-layouts: 27.2 us -> none  [per_device(): lax.scan(stats_step, fold_state, (key_blocks, value_blocks, offsets))]
    reduce_or x16 -> x0, other arithmetic: 20.7 us -> none  [the longest x8 10.5 us: stats_step(): jnp.any(visible)]
    reduce_sum x42 -> x0, other arithmetic: 12 us -> none  [the longest x8 8.86 us: stats_work(): jnp.sum(prob_block, axis=2)]
    another operation x18 -> x0, loops' own time: 11.5 us -> none  [the longest x1 5.34 us: per_device(): lax.scan(stats_step, fold_state, (key_blocks, value_blocks, offsets))]
  transfers between devices with their start and end apart: 4 -> 0, of which waited for: 4 -> 0; matrix products, arithmetic and copies ran while one was open for 2% -> 0% of each run, Pallas kernels for 0% -> 0%
where the time goes in v1:
time: 93.6 us; the launch traced here: 93.3 us
  Pallas kernels  85.6 us (91%)
  local copies, waits for them, and re-layouts  7.12 us (8%)
    pallas_call x1, Pallas kernels, per_device(): pl.pallas_call(kernel, out_shape=(jax.ShapeDtypeStruct(q.shape, BF16), ja...  85.6 us
    unnamed x15, local copies, waits for them, and re-layouts  7.12 us

profile of v1, /device:TPU:1, one launch (start us, length us, event | category | flops | bytes accessed | tf_op | source)
XLA Modules:
  0.0 93.3 jit_solution(8105175826894706349)
XLA Ops:
  0.6 0.0 copy-start
  0.6 1.0 %copy-done = bf16[128,2048]{1,0:T(8,128)(2,1)S(1)} copy-done((bf16[128,2048]{1,0:T(8,128)(2,1)S(1)}, bf16[128,2048]{1,0:T(8,128)(2,1)}, u32[]{:S(2)}) %copy-start) | copy-done | bytes 524312
  1.7 0.0 copy-start.1
  1.7 1.0 %copy-done.1 = bf16[128,2048]{1,0:T(8,128)(2,1)S(1)} copy-done((bf16[128,2048]{1,0:T(8,128)(2,1)S(1)}, bf16[128,2048]{1,0:T(8,128)(2,1)}, u32[]{:S(2)}) %copy-start.1) | copy-done | bytes 524312
  2.7 0.0 copy-start.2
  2.7 0.8 copy-done.2
  3.6 0.0 copy-start.3
  3.6 0.8 copy-done.3
  4.4 0.0 copy-start.4
  4.4 0.7 copy-done.4
  5.1 0.0 copy-start.5
  5.1 0.7 copy-done.5
  5.7 85.6 %shard_map.85 = (bf16[128,2048]{1,0:T(8,128)(2,1)S(1)}, bf16[128,256]{1,0:T(8,128)(2,1)S(1)}, bf16[128,256]{1,0:T(8,128)(2,1)S(1)}) custom-call(bf16[128,2048]{1,0:T(8,128)(2,1)S(1)} %copy-done, bf16[128,256]{1,0:T(8,128)(2,1)S(1)} %copy-done.2, bf16[128,256]{1,0:T(8,128)(2,1)S(1)} %copy-done.3, bf16[128,2048]{1,0:T(8,128)(2,1)S(1)} %copy-done.1, ...), custom_call_target="tpu_custom_call" | custom-call | tf_op jit(solution)/shard_map/pallas_call | solution.py:478
  91.3 0.8 copy.12
  92.1 0.6 copy.13
  92.7 0.6 copy.14
Async XLA Ops:
  0.6 1.0 %copy-start = (bf16[128,2048]{1,0:T(8,128)(2,1)S(1)}, bf16[128,2048]{1,0:T(8,128)(2,1)}, u32[]{:S(2)}) copy-start(bf16[128,2048]{1,0:T(8,128)(2,1)} %q_ref.1) | copy-start | bytes 1572868
  1.7 1.0 %copy-start.1 = (bf16[128,2048]{1,0:T(8,128)(2,1)S(1)}, bf16[128,2048]{1,0:T(8,128)(2,1)}, u32[]{:S(2)}) copy-start(bf16[128,2048]{1,0:T(8,128)(2,1)} %g_ref.1) | copy-start | bytes 1572868
  2.7 0.8 copy-start.2
  3.6 0.8 copy-start.3
  4.4 0.7 copy-start.4
  5.1 0.7 copy-start.5

commit v2 on v1

--- a/solution.py
+++ b/solution.py
@@ -57,22 +57,24 @@
     def zat(k):
         return lax.rem(z + k, LINE)
 
-    used = [0]
-
-    def remote(src, dst, target):
-        i = used[0]
-        used[0] = i + 1
+    def remote(src, dst, target, sent, got=None):
         return pltpu.make_async_remote_copy(
-            src_ref=src, dst_ref=dst, send_sem=send_sem.at[i], recv_sem=recv_sem.at[i],
+            src_ref=src, dst_ref=dst, send_sem=send_sem.at[sent],
+            recv_sem=recv_sem.at[sent if got is None else got],
             device_id=target, device_id_type=MESH,
         )
 
+    def z_turn(n):
+        return lax.rem(z + (1 + 2 * lax.div(z, 2)) * n, LINE)
+
+    def turn_of(there, source):
+        return lax.rem((1 + 2 * lax.div(there, 2)) * (source - there + LINE), LINE)
+
     right, left = device(xat(1), z, core), device(xat(RING - 1), z, core)
     brother = device(x, z, sib)
-    along_z = [None] + [device(x, zat(k), core) for k in range(1, LINE)]
 
     barrier = pltpu.get_barrier_semaphore()
-    peers = [brother, right, left] + along_z[1:]
+    peers = [brother, right, left] + [device(x, zat(k), core) for k in range(1, LINE)]
     for peer in peers:
         pl.semaphore_signal(barrier, inc=1, device_id=peer, device_id_type=MESH)
     pl.semaphore_wait(barrier, len(peers))
@@ -84,10 +86,10 @@
     own_rows, sib_rows = lanes(core, 128), lanes(sib, 128)
     wide = GROUP_HEADS * HEAD_SIZE
     swaps = [
-        remote(k_ref.at[:, lanes(sib, 128)], kv.at[mine, 0, own_rows, :], brother),
-        remote(v_ref.at[:, lanes(sib, 128)], kv.at[mine, 1, own_rows, :], brother),
-        remote(q_ref.at[:, lanes(sib, wide)], qin.at[1], brother),
-        remote(g_ref.at[:, lanes(sib, wide)], gin.at[1], brother),
+        remote(k_ref.at[:, lanes(sib, 128)], kv.at[mine, 0, own_rows, :], brother, SWAP),
+        remote(v_ref.at[:, lanes(sib, 128)], kv.at[mine, 1, own_rows, :], brother, SWAP + 1),
+        remote(q_ref.at[:, lanes(sib, wide)], qin.at[1], brother, SWAP + 2),
+        remote(g_ref.at[:, lanes(sib, wide)], gin.at[1], brother, SWAP + 3),
     ]
     for swap in swaps:
         swap.start()
@@ -107,43 +109,39 @@
     def slot(xx, zz):
         return zz * RING + xx
 
-    zsend = [None] + [remote(kv.at[mine], kv.at[mine], along_z[k]) for k in range(1, LINE)]
-    xright = [remote(kv.at[slot(x, zat(k))], kv.at[slot(x, zat(k))], right) for k in range(LINE)]
-    xleft = [remote(kv.at[slot(x, zat(k))], kv.at[slot(x, zat(k))], left) for k in range(LINE)]
-    fright = [
-        remote(kv.at[slot(xat(RING - 1), zat(k)), 0], kv.at[slot(xat(RING - 1), zat(k)), 0], right)
-        for k in range(LINE)
-    ]
-    fleft = [
-        remote(kv.at[slot(xat(1), zat(k)), 1], kv.at[slot(xat(1), zat(k)), 1], left)
-        for k in range(LINE)
-    ]
-    order = [0, LINE - 1, 1, 2]
-    xright[0].start()
-    xleft[0].start()
+    def z_copy(k):
+        there = zat(k)
+        return remote(
+            kv.at[mine], kv.at[mine], device(x, there, core), ZED + k, ZED + turn_of(there, z)
+        )
+
+    def z_wait(n):
+        block = kv.at[slot(x, z_turn(n))]
+        remote(block, block, right, ZED + n).wait_recv()
+
+    def x_copies(n):
+        block = kv.at[slot(x, z_turn(n))]
+        return remote(block, block, right, XR + n), remote(block, block, left, XL + n)
+
+    def relay_copies(n):
+        block_k = kv.at[slot(xat(RING - 1), z_turn(n)), 0]
+        block_v = kv.at[slot(xat(1), z_turn(n)), 1]
+        return remote(block_k, block_k, right, FR + n), remote(block_v, block_v, left, FL + n)
+
+    def start_x(n):
+        for copy in x_copies(n):
+            copy.start()
+
+    def relay(n):
+        for arrived, onward in zip(x_copies(n), relay_copies(n)):
+            arrived.wait_recv()
+            onward.start()
+
+    start_x(0)
     for k in (1, LINE - 1, 2):
-        zsend[k].start()
-
-    def relay(k):
-        xright[k].wait_recv()
-        fright[k].start()
-        xleft[k].wait_recv()
-        fleft[k].start()
-
-    for n, k in enumerate(order):
-        if n > 0:
-            zsend[LINE - k].wait_recv()
-            xright[k].start()
-            xleft[k].start()
-            relay(order[n - 1])
-    relay(order[-1])
-    for k in order:
-        fright[k].wait_recv()
-        fleft[k].wait_recv()
+        z_copy(k).start()
     own[2].wait()
     own[3].wait()
-    swaps[2].wait_recv()
-    swaps[3].wait_recv()
 
     pairs = [2 * chip + core, 2 * chip + sib]
 
@@ -159,6 +157,9 @@
     sub_row = lax.broadcasted_iota(jnp.int32, (8, COLS), 0)
     for p in range(2):
         small, flag = pair_small(pairs[p])
+        if p == 1:
+            swaps[2].wait_recv()
+            swaps[3].wait_recv()
         for side in range(2):
             turned = flag == 1 - side
             for h in range(GROUP_HEADS):
@@ -171,18 +172,15 @@
             for j in range(15 - RWIN + 1):
                 first = jnp.where(base + lane_row >= ends[j + RWIN - 1], ends[j], first)
             start[p, side] = first - sub_row
-            stats[0, p, side] = jnp.full((8, COLS), FAR, F32)
-            stats[1, p, side] = jnp.zeros((8, COLS), F32)
-            stats[2, p, side] = jnp.zeros((8, COLS), F32)
         dqacc[p] = jnp.zeros((COLS, 256), F32)
 
     eight = 8 * lax.broadcasted_iota(jnp.int32, (8, 8, COLS), 0)
     never = 1 << 20
 
-    def load_pairs(first_slot, slots):
+    def load_pairs(slots):
         small_k, large_k, small_v, large_v, firsts, flags = [], [], [], [], [], []
-        for t in range(2 * slots):
-            at = first_slot + t // 2
+        for t in range(2 * len(slots)):
+            at = slots[t // 2]
             pair = (lax.rem(at, RING) * LINE + lax.div(at, RING)) * 2 + t % 2
             small, flag = pair_small(pair)
             row = (t % 2) * 128
@@ -245,8 +243,8 @@
                 stats[n, p, 0] = jnp.where(sel, new, stats[n, p, 0])
                 stats[n, p, 1] = jnp.where(sel, old, new)
 
-    def stats_pass(first_slot, slots):
-        loaded = load_pairs(first_slot, slots)
+    def stats_pass(slots):
+        loaded = load_pairs(slots)
         for p in range(2):
             for keys, values, tiles, first_side in units(loaded, p):
                 scores, dprobs = products(p, keys, values, first_side)
@@ -285,8 +283,8 @@
         dqacc[p, :, width] += mul_tn(dscores_b, keys)
         return mul_nn(dscores_b, qcat[p, :, width]), mul_nn(probs_b, gcat[p, :, width])
 
-    def grad_pass(first_slot, slots):
-        loaded = load_pairs(first_slot, slots)
+    def grad_pass(slots):
+        loaded = load_pairs(slots)
         flags = loaded[-1]
         small = [0.0, 0.0]
         large = [0.0, 0.0]
@@ -309,7 +307,7 @@
         for n in range(2):
             for t, flag in enumerate(flags):
                 rows = slice(t * HALF, (t + 1) * HALF)
-                at, row = first_slot + t // 2, (t % 2) * 128
+                at, row = slots[t // 2], (t % 2) * 128
                 turned = flag == 1
                 lo, hi = small[n][rows], large[n][rows]
                 part[at, n, row : row + HALF, :] = jnp.where(turned, hi, lo)
@@ -357,11 +355,22 @@
             stats[1, p, side] = jnp.sum(probs, axis=0)
             stats[2, p, side] = jnp.sum(probs * dprobs[rows].reshape(8, 8, COLS), axis=0)
 
-    tile_slots = 2
-
-    @pl.loop(0, RING * LINE // tile_slots)
+    z_wait(1)
+    start_x(1)
+
+    @pl.loop(0, LINE)
     def _(n):
-        stats_pass(n * tile_slots, tile_slots)
+        @pl.when(n < LINE - 2)
+        def _():
+            z_wait(n + 2)
+            start_x(n + 2)
+
+        relay(n)
+        zz = z_turn(n)
+        stats_pass([slot(x, zz), slot(xat(1), zz)])
+        for copy in relay_copies(n):
+            copy.wait_recv()
+        stats_pass([slot(xat(RING - 1), zz), slot(xat(2), zz)])
 
     for p in range(2):
         for side in range(2):
@@ -373,9 +382,56 @@
             stats[0, p, side] = jnp.broadcast_to(best + jnp.log2(total), (8, COLS))
             stats[1, p, side] = jnp.broadcast_to(weighted / total, (8, COLS))
 
-    @pl.loop(0, RING * LINE // tile_slots)
-    def _(n):
-        grad_pass(n * tile_slots, tile_slots)
+    def far_copies(n):
+        return remote(s1r.at[n], r1l.at[n], right, C1R + n), remote(s1l.at[n], r1r.at[n], left, C1L + n)
+
+    def near_copies(n):
+        return remote(s2r.at[n], r2l.at[n], right, C2R + n), remote(s2l.at[n], r2r.at[n], left, C2L + n)
+
+    def last_copy(n):
+        there = z_turn(n)
+        turn = turn_of(there, z)
+        return remote(s3.at[n], r3.at[turn], device(x, there, core), C3 + n, C3 + turn)
+
+    def send_far(n):
+        far = slot(xat(2), z_turn(n))
+        s1r[n] = part[far, 0].astype(BF16)
+        s1l[n] = part[far, 1].astype(BF16)
+        for copy in far_copies(n):
+            copy.start()
+
+    def send_near(n):
+        to_right, to_left = slot(xat(1), z_turn(n)), slot(xat(RING - 1), z_turn(n))
+        arrived = far_copies(n)
+        onward = near_copies(n)
+        s2r[n, 1] = part[to_right, 1].astype(BF16)
+        s2l[n, 0] = part[to_left, 0].astype(BF16)
+        arrived[0].wait_recv()
+        s2r[n, 0] = (part[to_right, 0] + r1l[n].astype(F32)).astype(BF16)
+        onward[0].start()
+        arrived[1].wait_recv()
+        s2l[n, 1] = (part[to_left, 1] + r1r[n].astype(F32)).astype(BF16)
+        onward[1].start()
+
+    def x_total(n):
+        for copy in near_copies(n):
+            copy.wait_recv()
+        return part[slot(x, z_turn(n))] + r2l[n].astype(F32) + r2r[n].astype(F32)
+
+    @pl.loop(0, LINE)
+    def _(i):
+        n = LINE - 1 - i
+        zz = z_turn(n)
+        grad_pass([slot(xat(2), zz), slot(xat(1), zz)])
+        send_far(n)
+
+        @pl.when(i > 0)
+        def _():
+            s3[n + 1] = x_total(n + 1).astype(BF16)
+            last_copy(n + 1).start()
+
+        grad_pass([slot(xat(RING - 1), zz), slot(x, zz)])
+        send_near(n)
 
     for p in range(2):
         keys, values, masks, flag = own_tile(p)
@@ -398,52 +454,22 @@
             lo, hi = both[:, :128], both[:, 128:]
             dqout[p, :HALF, h * 128 : h * 128 + 128] = jnp.where(turned, hi, lo).astype(BF16)
             dqout[p, HALF:, h * 128 : h * 128 + 128] = jnp.where(turned, lo, hi).astype(BF16)
-    dq_out = remote(dqout.at[1], dq_ref.at[:, lanes(core, wide)], brother)
+    dq_out = remote(dqout.at[1], dq_ref.at[:, lanes(core, wide)], brother, DQ)
     dq_out.start()
     dq_own = pltpu.make_async_copy(dqout.at[0], dq_ref.at[:, lanes(core, wide)], local_sem.at[4])
     dq_own.start()
 
-    back = [LINE - 1, 2, 1, 0]
-    far_x = [xat(2), xat(1), xat(RING - 1), x]
-    c1r = [remote(s1r.at[k], r1l.at[k], right) for k in range(LINE)]
-    c1l = [remote(s1l.at[k], r1r.at[k], left) for k in range(LINE)]
-    c2r = [remote(s2r.at[k], r2l.at[k], right) for k in range(LINE)]
-    c2l = [remote(s2l.at[k], r2r.at[k], left) for k in range(LINE)]
-    c3 = [None] + [remote(s3.at[k], r3.at[k], along_z[k]) for k in range(1, LINE)]
-    for k in back:
-        s1r[k] = part[slot(far_x[0], zat(k)), 0].astype(BF16)
-        c1r[k].start()
-        s1l[k] = part[slot(far_x[0], zat(k)), 1].astype(BF16)
-        c1l[k].start()
-    for k in back:
-        to_right, to_left = slot(far_x[1], zat(k)), slot(far_x[2], zat(k))
-        s2r[k, 1] = part[to_right, 1].astype(BF16)
-        s2l[k, 0] = part[to_left, 0].astype(BF16)
-        c1r[k].wait_recv()
-        s2r[k, 0] = (part[to_right, 0] + r1l[k].astype(F32)).astype(BF16)
-        c2r[k].start()
-        c1l[k].wait_recv()
-        s2l[k, 1] = (part[to_left, 1] + r1r[k].astype(F32)).astype(BF16)
-        c2l[k].start()
-    for k in back:
-        c2r[k].wait_recv()
-        c2l[k].wait_recv()
-        whole = part[slot(x, zat(k))] + r2l[k].astype(F32) + r2r[k].astype(F32)
-        if k > 0:
-            s3[k] = whole.astype(BF16)
-            c3[k].start()
-        else:
-            part[mine] = whole
-    for k in range(1, LINE):
-        c3[k].wait_recv()
+    part[mine] = x_total(0)
+    for turn in range(1, LINE):
+        remote(s3.at[0], r3.at[turn], right, C3 + turn).wait_recv()
     for n, factor in ((0, SCALE), (1, 1.0)):
         whole = part[mine, n]
         for k in range(1, LINE):
             whole = whole + r3[k, n].astype(F32)
         fin[n] = (whole * factor).astype(BF16)
     outs = [
-        remote(fin.at[0, sib_rows, :], dk_ref.at[:, lanes(core, 128)], brother),
-        remote(fin.at[1, sib_rows, :], dv_ref.at[:, lanes(core, 128)], brother),
+        remote(fin.at[0, sib_rows, :], dk_ref.at[:, lanes(core, 128)], brother, OUT),
+        remote(fin.at[1, sib_rows, :], dv_ref.at[:, lanes(core, 128)], brother, OUT + 1),
     ]
     for out in outs:
         out.start()
@@ -459,13 +485,19 @@
     dq_out.wait_recv()
     for out in outs:
         out.wait_recv()
-    for copy in (
-        swaps + zsend[1:] + xright + xleft + fright + fleft + [dq_out] + c1r + c1l + c2r + c2l + c3[1:] + outs
-    ):
+    for copy in swaps + outs + [dq_out]:
         copy.wait_send()
-
-
-COPIES = 4 + 3 + 4 * LINE + 1 + 4 * LINE + 3 + 2
+    for n in range(LINE):
+        for copy in x_copies(n) + relay_copies(n) + far_copies(n) + near_copies(n):
+            copy.wait_send()
+    for n in range(1, LINE):
+        z_copy(n).wait_send()
+        last_copy(n).wait_send()
+
+
+SWAP, OUT, DQ, ZED = 0, 4, 6, 7
+XR, XL, FR, FL, C1R, C1L, C2R, C2L, C3 = range(ZED + LINE, ZED + 10 * LINE, LINE)
+COPIES = ZED + 10 * LINE
 
 
 def per_device(q, k, v, g, lengths, assignment):

time: 93.6 us -> 88.6 us (0.947)
  Pallas kernels: 85.6 us -> 80.6 us
    pallas_call x1, Pallas kernels: 85.6 us -> 80.6 us  [per_device(): pl.pallas_call(kernel, out_shape=(jax.ShapeDtypeStruct(q.shape, BF16), ja...]
where the time goes in v2:
time: 88.6 us; the launch traced here: 88.3 us
  Pallas kernels  80.6 us (91%)
  local copies, waits for them, and re-layouts  7.12 us (8%)
    pallas_call x1, Pallas kernels, per_device(): pl.pallas_call(kernel, out_shape=(jax.ShapeDtypeStruct(q.shape, BF16), ja...  80.6 us
    unnamed x15, local copies, waits for them, and re-layouts  7.12 us

profile of v2, /device:TPU:1, one launch (start us, length us, event | category | flops | bytes accessed | tf_op | source)
XLA Modules:
  0.0 88.3 jit_solution(15420940880669986328)
XLA Ops:
  0.6 0.0 copy-start
  0.6 1.0 %copy-done = bf16[128,2048]{1,0:T(8,128)(2,1)S(1)} copy-done((bf16[128,2048]{1,0:T(8,128)(2,1)S(1)}, bf16[128,2048]{1,0:T(8,128)(2,1)}, u32[]{:S(2)}) %copy-start) | copy-done | bytes 524312
  1.7 0.0 copy-start.1
  1.7 1.0 %copy-done.1 = bf16[128,2048]{1,0:T(8,128)(2,1)S(1)} copy-done((bf16[128,2048]{1,0:T(8,128)(2,1)S(1)}, bf16[128,2048]{1,0:T(8,128)(2,1)}, u32[]{:S(2)}) %copy-start.1) | copy-done | bytes 524312
  2.7 0.0 copy-start.2
  2.7 0.8 copy-done.2
  3.6 0.0 copy-start.3
  3.6 0.8 copy-done.3
  4.4 0.0 copy-start.4
  4.4 0.7 copy-done.4
  5.1 0.0 copy-start.5
  5.1 0.7 copy-done.5
  5.7 80.6 %shard_map.85 = (bf16[128,2048]{1,0:T(8,128)(2,1)S(1)}, bf16[128,256]{1,0:T(8,128)(2,1)S(1)}, bf16[128,256]{1,0:T(8,128)(2,1)S(1)}) custom-call(bf16[128,2048]{1,0:T(8,128)(2,1)S(1)} %copy-done, bf16[128,256]{1,0:T(8,128)(2,1)S(1)} %copy-done.2, bf16[128,256]{1,0:T(8,128)(2,1)S(1)} %copy-done.3, bf16[128,2048]{1,0:T(8,128)(2,1)S(1)} %copy-done.1, ...), custom_call_target="tpu_custom_call" | custom-call | tf_op jit(solution)/shard_map/pallas_call | solution.py:510
  86.3 0.8 copy.12
  87.1 0.6 copy.13
  87.7 0.6 copy.14
Async XLA Ops:
  0.6 1.0 %copy-start = (bf16[128,2048]{1,0:T(8,128)(2,1)S(1)}, bf16[128,2048]{1,0:T(8,128)(2,1)}, u32[]{:S(2)}) copy-start(bf16[128,2048]{1,0:T(8,128)(2,1)} %q_ref.1) | copy-start | bytes 1572868
  1.7 1.0 %copy-start.1 = (bf16[128,2048]{1,0:T(8,128)(2,1)S(1)}, bf16[128,2048]{1,0:T(8,128)(2,1)}, u32[]{:S(2)}) copy-start(bf16[128,2048]{1,0:T(8,128)(2,1)} %g_ref.1) | copy-start | bytes 1572868
  2.7 0.8 copy-start.2
  3.6 0.8 copy-start.3
  4.4 0.7 copy-start.4
  5.1 0.7 copy-start.5

commit v3 on v2

--- a/solution.py
+++ b/solution.py
@@ -65,10 +65,10 @@
         )
 
     def z_turn(n):
-        return lax.rem(z + (1 + 2 * lax.div(z, 2)) * n, LINE)
-
-    def turn_of(there, source):
-        return lax.rem((1 + 2 * lax.div(there, 2)) * (source - there + LINE), LINE)
+        low = jnp.minimum(z, LINE - 1 - z)
+        inner = jnp.where(n == 0, 1, jnp.where(n == 1, 2, jnp.where(n == 2, 0, 3)))
+        at = jnp.where(low == 0, n, inner)
+        return jnp.where(z >= LINE // 2, LINE - 1 - at, at)
 
     right, left = device(xat(1), z, core), device(xat(RING - 1), z, core)
     brother = device(x, z, sib)
@@ -101,47 +101,67 @@
     ]
     for copy in own:
         copy.start()
-    own[0].wait()
-    own[1].wait()
-    swaps[0].wait_recv()
-    swaps[1].wait_recv()
 
     def slot(xx, zz):
         return zz * RING + xx
 
-    def z_copy(k):
-        there = zat(k)
-        return remote(
-            kv.at[mine], kv.at[mine], device(x, there, core), ZED + k, ZED + turn_of(there, z)
+    up, down = device(x, jnp.minimum(z + 1, LINE - 1), core), device(x, jnp.maximum(z - 1, 0), core)
+
+    def z_piece(zz, n, target):
+        piece = kv.at[slot(x, zz), n]
+        return remote(piece, piece, target, ZED + 8 * n + zz, ZED + 8 * n + zz)
+
+    def z_onward(zz, n, do):
+        piece = kv.at[slot(x, zz), n]
+
+        @pl.when((zz <= z) & (z < LINE - 1))
+        def _():
+            do(remote(piece, piece, up, ZED + 8 * n + zz))
+
+        @pl.when((zz >= z) & (z > 0))
+        def _():
+            do(remote(piece, piece, down, ZED + 8 * n + 4 + zz, ZED + 8 * n + zz))
+
+    def x_piece(zz, n):
+        piece = kv.at[slot(x, zz), n]
+        return (
+            remote(piece, piece, right, XR + 4 * n + zz),
+            remote(piece, piece, left, XL + 4 * n + zz),
         )
 
-    def z_wait(n):
-        block = kv.at[slot(x, z_turn(n))]
-        remote(block, block, right, ZED + n).wait_recv()
-
-    def x_copies(n):
-        block = kv.at[slot(x, z_turn(n))]
-        return remote(block, block, right, XR + n), remote(block, block, left, XL + n)
-
-    def relay_copies(n):
-        block_k = kv.at[slot(xat(RING - 1), z_turn(n)), 0]
-        block_v = kv.at[slot(xat(1), z_turn(n)), 1]
-        return remote(block_k, block_k, right, FR + n), remote(block_v, block_v, left, FL + n)
-
-    def start_x(n):
-        for copy in x_copies(n):
+    def relay_copies(zz):
+        piece_k = kv.at[slot(xat(RING - 1), zz), 0]
+        piece_v = kv.at[slot(xat(1), zz), 1]
+        return remote(piece_k, piece_k, right, FR + zz), remote(piece_v, piece_v, left, FL + zz)
+
+    def send_piece(zz, n):
+        for copy in x_piece(zz, n):
             copy.start()
-
-    def relay(n):
-        for arrived, onward in zip(x_copies(n), relay_copies(n)):
-            arrived.wait_recv()
-            onward.start()
-
-    start_x(0)
-    for k in (1, LINE - 1, 2):
-        z_copy(k).start()
-    own[2].wait()
-    own[3].wait()
+        z_onward(zz, n, lambda copy: copy.start())
+
+    def z_step(turn):
+        zz = z_turn(turn)
+        for n in range(2):
+            z_piece(zz, n, up).wait_recv()
+            send_piece(zz, n)
+
+    def relay(turn):
+        zz = z_turn(turn)
+        onward = relay_copies(zz)
+        x_piece(zz, 0)[0].wait_recv()
+        onward[0].start()
+        x_piece(zz, 1)[1].wait_recv()
+        onward[1].start()
+
+    def rest_of_x(turn):
+        zz = z_turn(turn)
+        x_piece(zz, 0)[1].wait_recv()
+        x_piece(zz, 1)[0].wait_recv()
+
+    for n in range(2):
+        own[n].wait()
+        swaps[n].wait_recv()
+        send_piece(z, n)
 
     pairs = [2 * chip + core, 2 * chip + sib]
 
@@ -157,7 +177,11 @@
     sub_row = lax.broadcasted_iota(jnp.int32, (8, COLS), 0)
     for p in range(2):
         small, flag = pair_small(pairs[p])
-        if p == 1:
+        if p == 0:
+            own[2].wait()
+            own[3].wait()
+        else:
+            z_step(1)
             swaps[2].wait_recv()
             swaps[3].wait_recv()
         for side in range(2):
@@ -344,6 +368,9 @@
         return side == 0
 
     for p in range(2):
+        relay(p)
+        if p == 1:
+            z_step(2)
         keys, values, masks, unused_flag = own_tile(p)
         scores, dprobs = products(p, keys, values, 0)
         for side in range(2):
@@ -355,22 +382,23 @@
             stats[1, p, side] = jnp.sum(probs, axis=0)
             stats[2, p, side] = jnp.sum(probs * dprobs[rows].reshape(8, 8, COLS), axis=0)
 
-    z_wait(1)
-    start_x(1)
-
     @pl.loop(0, LINE)
-    def _(n):
-        @pl.when(n < LINE - 2)
+    def _(turn):
+        rest_of_x(turn)
+        zz = z_turn(turn)
+        stats_pass([slot(x, zz), slot(xat(1), zz)])
+
+        @pl.when(turn == 0)
         def _():
-            z_wait(n + 2)
-            start_x(n + 2)
-
-        relay(n)
-        zz = z_turn(n)
-        stats_pass([slot(x, zz), slot(xat(1), zz)])
-        for copy in relay_copies(n):
+            z_step(LINE - 1)
+
+        for copy in relay_copies(zz):
             copy.wait_recv()
         stats_pass([slot(xat(RING - 1), zz), slot(xat(2), zz)])
+
+        @pl.when(turn < LINE - 2)
+        def _():
+            relay(turn + 2)
 
     for p in range(2):
         for side in range(2):
@@ -389,19 +417,19 @@
         return remote(s2r.at[n], r2l.at[n], right, C2R + n), remote(s2l.at[n], r2r.at[n], left, C2L + n)
 
     def last_copy(n):
-        there = z_turn(n)
-        turn = turn_of(there, z)
-        return remote(s3.at[n], r3.at[turn], device(x, there, core), C3 + n, C3 + turn)
-
-    def send_far(n):
-        far = slot(xat(2), z_turn(n))
+        return remote(s3.at[n], r3.at[z], device(x, n, core), C3 + n, C3 + z)
+
+    def send_far(turn):
+        n = z_turn(turn)
+        far = slot(xat(2), n)
         s1r[n] = part[far, 0].astype(BF16)
         s1l[n] = part[far, 1].astype(BF16)
         for copy in far_copies(n):
             copy.start()
 
-    def send_near(n):
-        to_right, to_left = slot(xat(1), z_turn(n)), slot(xat(RING - 1), z_turn(n))
+    def send_near(turn):
+        n = z_turn(turn)
+        to_right, to_left = slot(xat(1), n), slot(xat(RING - 1), n)
         arrived = far_copies(n)
         onward = near_copies(n)
         s2r[n, 1] = part[to_right, 1].astype(BF16)
@@ -416,24 +444,33 @@
     def x_total(n):
         for copy in near_copies(n):
             copy.wait_recv()
-        return part[slot(x, z_turn(n))] + r2l[n].astype(F32) + r2r[n].astype(F32)
+        return part[slot(x, n)] + r2l[n].astype(F32) + r2r[n].astype(F32)
+
+    def send_last(turn):
+        n = z_turn(turn)
+        s3[n] = x_total(n).astype(BF16)
+        last_copy(n).start()
 
     @pl.loop(0, LINE)
     def _(i):
-        n = LINE - 1 - i
-        zz = z_turn(n)
+        turn = LINE - 1 - i
+        zz = z_turn(turn)
         grad_pass([slot(xat(2), zz), slot(xat(1), zz)])
-        send_far(n)
+        send_far(turn)
 
         @pl.when(i > 0)
         def _():
-            s3[n + 1] = x_total(n + 1).astype(BF16)
-            last_copy(n + 1).start()
+            send_near(turn + 1)
 
         grad_pass([slot(xat(RING - 1), zz), slot(x, zz)])
-        send_near(n)
+
+        @pl.when(i > 1)
+        def _():
+            send_last(turn + 2)
 
     for p in range(2):
+        if p == 1:
+            send_near(0)
         keys, values, masks, flag = own_tile(p)
         tiles = [(True, masks[0]), (False, masks[1])]
         grads = grad_tile(p, keys, values, tiles, 0)
@@ -445,6 +482,8 @@
                 [jnp.where(turned, hi, lo), jnp.where(turned, lo, hi)], axis=0
             )
             part[mine, n, rows, :] += dextra[...]
+
+    send_last(1)
 
     for p in range(2):
         unused_small, flag = pair_small(pairs[p])
@@ -459,13 +498,14 @@
     dq_own = pltpu.make_async_copy(dqout.at[0], dq_ref.at[:, lanes(core, wide)], local_sem.at[4])
     dq_own.start()
 
-    part[mine] = x_total(0)
-    for turn in range(1, LINE):
-        remote(s3.at[0], r3.at[turn], right, C3 + turn).wait_recv()
+    part[mine] = x_total(z)
+    for k in range(1, LINE):
+        there = zat(k)
+        remote(s3.at[0], r3.at[there], right, C3 + there).wait_recv()
     for n, factor in ((0, SCALE), (1, 1.0)):
         whole = part[mine, n]
         for k in range(1, LINE):
-            whole = whole + r3[k, n].astype(F32)
+            whole = whole + r3[zat(k), n].astype(F32)
         fin[n] = (whole * factor).astype(BF16)
     outs = [
         remote(fin.at[0, sib_rows, :], dk_ref.at[:, lanes(core, 128)], brother, OUT),
@@ -488,22 +528,22 @@
     for copy in swaps + outs + [dq_out]:
         copy.wait_send()
     for n in range(LINE):
-        for copy in x_copies(n) + relay_copies(n) + far_copies(n) + near_copies(n):
+        for copy in x_piece(n, 0) + x_piece(n, 1) + relay_copies(n) + far_copies(n) + near_copies(n):
             copy.wait_send()
-    for n in range(1, LINE):
-        z_copy(n).wait_send()
-        last_copy(n).wait_send()
-
-
-SWAP, OUT, DQ, ZED = 0, 4, 6, 7
-XR, XL, FR, FL, C1R, C1L, C2R, C2L, C3 = range(ZED + LINE, ZED + 10 * LINE, LINE)
-COPIES = ZED + 10 * LINE
+        for piece in range(2):
+            z_onward(n, piece, lambda copy: copy.wait_send())
+    for k in range(1, LINE):
+        last_copy(zat(k)).wait_send()
+
+
+SWAP, OUT, DQ, ZED, XR, XL = 0, 4, 6, 8, 24, 32
+FR, FL, C1R, C1L, C2R, C2L, C3 = range(40, 40 + 7 * LINE, LINE)
+COPIES = 40 + 7 * LINE
 
 
 def per_device(q, k, v, g, lengths, assignment):
     slots = RING * LINE
     anywhere = pl.BlockSpec(memory_space=pl.ANY)
-    vmem = pl.BlockSpec(memory_space=pltpu.VMEM)
     smem = pl.BlockSpec(memory_space=pltpu.SMEM)
     half = (LINE, 256, 128)
     full = (LINE, 2, 256, 128)
@@ -515,7 +555,7 @@
             jax.ShapeDtypeStruct(v.shape, BF16),
         ),
         in_specs=[anywhere] * 4 + [smem] * 2,
-        out_specs=(vmem, vmem, vmem),
+        out_specs=(anywhere, anywhere, anywhere),
         scratch_shapes=[
             pltpu.VMEM((slots, 2, 256, 128), BF16),
             pltpu.VMEM((2, 128, 1024), BF16),
@@ -544,7 +584,7 @@
             pltpu.SemaphoreType.DMA((COPIES,)),
         ],
         compiler_params=pltpu.CompilerParams(
-            collective_id=0, has_side_effects=True, vmem_limit_bytes=50 * 1024 * 1024
+            collective_id=0, has_side_effects=True, vmem_limit_bytes=63 * 1024 * 1024
         ),
     )(q, k, v, g, lengths, assignment)
 

time: 88.6 us -> 65 us (0.73)
  Pallas kernels: 80.6 us -> 60.1 us
  local copies, waits for them, and re-layouts: 7.12 us -> 3.41 us
    pallas_call x1, Pallas kernels: 80.6 us -> 60.1 us  [per_device(): pl.pallas_call(kernel, out_shape=(jax.ShapeDtypeStruct(q.shape, BF16), ja...]
    unnamed x15 -> x7, local copies, waits for them, and re-layouts: 7.12 us -> 3.41 us
where the time goes in v3:
time: 65 us; the launch traced here: 64.2 us
  Pallas kernels  60.1 us (92%)
  local copies, waits for them, and re-layouts  3.41 us (5%)
  between operations  0.65 us (1%)
    pallas_call x1, Pallas kernels, per_device(): pl.pallas_call(kernel, out_shape=(jax.ShapeDtypeStruct(q.shape, BF16), ja...  60.1 us
    unnamed x7, local copies, waits for them, and re-layouts  3.41 us

profile of v3, /device:TPU:1, one launch (start us, length us, event | category | flops | bytes accessed | tf_op | source)
XLA Modules:
  0.0 64.2 jit_solution(12220683220670150950)
XLA Ops:
  0.6 60.1 %shard_map.85 = (bf16[128,2048]{1,0:T(8,128)(2,1)}, bf16[128,256]{1,0:T(8,128)(2,1)}, bf16[128,256]{1,0:T(8,128)(2,1)}) custom-call(bf16[128,2048]{1,0:T(8,128)(2,1)} %q_ref.1, bf16[128,256]{1,0:T(8,128)(2,1)} %k_ref.1, bf16[128,256]{1,0:T(8,128)(2,1)} %v_ref.1, bf16[128,2048]{1,0:T(8,128)(2,1)} %g_ref.1, s32[16]{0:T(128)} %len_ref.1, s32[64]{0:T(128)} %asg_ref.1), custom_call_target="tpu_custom_call" | custom-call | tf_op jit(solution)/shard_map/pallas_call | solution.py:550
  60.8 0.0 copy-start.1
  60.8 1.9 %copy.12 = bf16[128,2048]{1,0:T(8,128)(2,1)} copy(bf16[128,2048]{1,0:T(8,128)(2,1)} %get-tuple-element.6) | data formatting | bytes 1048576
  62.7 0.0 copy-done.1
  62.7 0.0 copy-start
  62.7 0.6 copy.13
  63.3 0.2 copy-done
  63.6 0.6 copy.14
Async XLA Ops:
  60.8 1.9 %copy-start.1 = (bf16[128,256]{1,0:T(8,128)(2,1)S(1)}, bf16[128,256]{1,0:T(8,128)(2,1)}, u32[]{:S(2)}) copy-start(bf16[128,256]{1,0:T(8,128)(2,1)} %get-tuple-element.7) | copy-start | bytes 196612
  62.7 0.9 %copy-start = (bf16[128,256]{1,0:T(8,128)(2,1)S(1)}, bf16[128,256]{1,0:T(8,128)(2,1)}, u32[]{:S(2)}) copy-start(bf16[128,256]{1,0:T(8,128)(2,1)} %get-tuple-element.8) | copy-start | bytes 196612

commit v4 on v3

--- a/solution.py
+++ b/solution.py
@@ -40,7 +40,7 @@
     dq_ref, dk_ref, dv_ref,
     kv, qin, gin, qcat, gcat, stats, start, dqacc, part, dextra, dqout, fin,
     s1r, s1l, r1l, r1r, s2r, s2l, r2l, r2r, s3, r3,
-    local_sem, send_sem, recv_sem,
+    saved, local_sem, send_sem, recv_sem,
 ):
     blocks = asg_ref.shape[0]
     me = lax.axis_index("round")
@@ -196,7 +196,7 @@
             for j in range(15 - RWIN + 1):
                 first = jnp.where(base + lane_row >= ends[j + RWIN - 1], ends[j], first)
             start[p, side] = first - sub_row
-        dqacc[p] = jnp.zeros((COLS, 256), F32)
+        dqacc[p] = jnp.zeros((256, COLS), F32)
 
     eight = 8 * lax.broadcasted_iota(jnp.int32, (8, 8, COLS), 0)
     never = 1 << 20
@@ -249,8 +249,7 @@
         width = slice(128, 256) if first_side == 1 else slice(0, 256)
         return mul_nt(keys, qcat[p, :, width]), mul_nt(values, gcat[p, :, width])
 
-    def stats_unit(p, sel, mask, scores, dprobs):
-        scores = jnp.where(mask, scores * SCALE2, FAR)
+    def stats_unit(p, sel, scores, dprobs):
         top = side_of(sel, lambda side: stats[0, p, side])
         new_top = jnp.maximum(top, jnp.max(scores, axis=0))
         rescale = jnp.exp2(top - new_top)
@@ -267,62 +266,61 @@
                 stats[n, p, 0] = jnp.where(sel, new, stats[n, p, 0])
                 stats[n, p, 1] = jnp.where(sel, old, new)
 
-    def stats_pass(slots):
+    def stats_pass(at, slots):
         loaded = load_pairs(slots)
         for p in range(2):
-            for keys, values, tiles, first_side in units(loaded, p):
+            for ab, (keys, values, tiles, first_side) in enumerate(units(loaded, p)):
                 scores, dprobs = products(p, keys, values, first_side)
+                saved[at, p, ab, 1] = dprobs
                 for t, (sel, begin) in enumerate(tiles):
                     rows = slice(t * HALF, (t + 1) * HALF)
-                    stats_unit(
-                        p, sel, eight >= begin[None],
-                        scores[rows].reshape(8, 8, COLS), dprobs[rows].reshape(8, 8, COLS),
-                    )
-
-    def grad_unit(p, sel, mask, scores, dprobs):
-        scores = jnp.where(mask, scores * SCALE2, FAR)
+                    mask = eight >= begin[None]
+                    masked = jnp.where(mask, scores[rows].reshape(8, 8, COLS) * SCALE2, FAR)
+                    saved[at, p, ab, 0, rows] = masked.reshape(HALF, COLS)
+                    stats_unit(p, sel, masked, dprobs[rows].reshape(8, 8, COLS))
+
+    def grad_unit(p, sel, scores, dprobs):
         log_total = side_of(sel, lambda side: stats[0, p, side])
         delta = side_of(sel, lambda side: stats[1, p, side])
-        probs = jnp.exp2(scores - log_total[None])
-        dscores = probs * (dprobs - delta[None])
+        probs = jnp.exp2(scores.reshape(8, 8, COLS) - log_total[None])
+        dscores = probs * (dprobs.reshape(8, 8, COLS) - delta[None])
         return (
             probs.reshape(HALF, COLS).astype(BF16),
             dscores.reshape(HALF, COLS).astype(BF16),
         )
 
-    def grad_tile(p, keys, values, tiles, first_side):
+    def grad_tile(p, keys_t, sels, first_side, load):
         width = slice(128, 256) if first_side == 1 else slice(0, 256)
-        scores, dprobs = products(p, keys, values, first_side)
         probs_b, dscores_b = [], []
-        for t, (sel, mask) in enumerate(tiles):
-            rows = slice(t * HALF, (t + 1) * HALF)
-            one, two = grad_unit(
-                p, sel, mask,
-                scores[rows].reshape(8, 8, COLS), dprobs[rows].reshape(8, 8, COLS),
-            )
+        for t, sel in enumerate(sels):
+            one, two = grad_unit(p, sel, *load(slice(t * HALF, (t + 1) * HALF)))
             probs_b.append(one)
             dscores_b.append(two)
         probs_b = jnp.concatenate(probs_b, axis=0)
         dscores_b = jnp.concatenate(dscores_b, axis=0)
-        dqacc[p, :, width] += mul_tn(dscores_b, keys)
+        dqacc[p, width, :] += mul_nn(keys_t, dscores_b)
         return mul_nn(dscores_b, qcat[p, :, width]), mul_nn(probs_b, gcat[p, :, width])
 
-    def grad_pass(slots):
-        loaded = load_pairs(slots)
-        flags = loaded[-1]
+    def grad_pass(at, slots):
+        small_k, large_k, unused_v, unused_w, firsts, flags = load_pairs(slots)
         small = [0.0, 0.0]
         large = [0.0, 0.0]
+        small_t = jnp.concatenate(small_k, axis=0).T
         for p in range(2):
-            (ka, va, ta, unused_a), (kb, vb, tb, unused_b) = units(loaded, p)
-            ta = [(sel, eight >= begin[None]) for sel, begin in ta]
-            masks_b = [(sel, eight >= begin[None]) for sel, begin in tb]
-            grads_a = grad_tile(p, ka, va, ta, 1)
-            grads_b = grad_tile(p, kb, vb, masks_b, 0)
+            mine_small, unused_flag = pair_small(pairs[p])
+            sels = [j < mine_small for j in firsts]
+            both_t = jnp.concatenate([halves(*b) for b in zip(sels, small_k, large_k)], axis=0).T
+
+            def load(ab):
+                return lambda rows: (saved[at, p, ab, 0, rows], saved[at, p, ab, 1, rows])
+
+            grads_a = grad_tile(p, small_t, [None] * len(sels), 1, load(0))
+            grads_b = grad_tile(p, both_t, sels, 0, load(1))
             for n in range(2):
                 small[n] = small[n] + grads_a[n]
                 zero = jnp.zeros((HALF, 128), F32)
                 add_small, add_large = [], []
-                for t, (sel, unused_mask) in enumerate(tb):
+                for t, sel in enumerate(sels):
                     rows = slice(t * HALF, (t + 1) * HALF)
                     add_small.append(jnp.where(sel, grads_b[n][rows, :128], zero))
                     add_large.append(jnp.where(sel, zero, grads_b[n][rows, 128:]))
@@ -331,11 +329,11 @@
         for n in range(2):
             for t, flag in enumerate(flags):
                 rows = slice(t * HALF, (t + 1) * HALF)
-                at, row = slots[t // 2], (t % 2) * 128
+                at_slot, row = slots[t // 2], (t % 2) * 128
                 turned = flag == 1
                 lo, hi = small[n][rows], large[n][rows]
-                part[at, n, row : row + HALF, :] = jnp.where(turned, hi, lo)
-                part[at, n, row + HALF : row + 128, :] = jnp.where(turned, lo, hi)
+                part[at_slot, n, row : row + HALF, :] = jnp.where(turned, hi, lo)
+                part[at_slot, n, row + HALF : row + 128, :] = jnp.where(turned, lo, hi)
 
     tri = lax.broadcasted_iota(jnp.int32, (8, 8, COLS), 1) + eight <= lax.rem(
         lax.broadcasted_iota(jnp.int32, (8, 8, COLS), 2), HALF
@@ -363,9 +361,6 @@
             base = (small if side == 0 else blocks - 1 - small) * HALF
             masks.append(tri & (eight >= (start[p, side] - base)[None]))
         return stack(0), stack(1), masks, flag
-
-    def side_const(side):
-        return side == 0
 
     for p in range(2):
         relay(p)
@@ -386,7 +381,7 @@
     def _(turn):
         rest_of_x(turn)
         zz = z_turn(turn)
-        stats_pass([slot(x, zz), slot(xat(1), zz)])
+        stats_pass(2 * zz + 1, [slot(xat(RING - 1), zz), slot(x, zz)])
 
         @pl.when(turn == 0)
         def _():
@@ -394,7 +389,7 @@
 
         for copy in relay_copies(zz):
             copy.wait_recv()
-        stats_pass([slot(xat(RING - 1), zz), slot(xat(2), zz)])
+        stats_pass(2 * zz, [slot(xat(2), zz), slot(xat(1), zz)])
 
         @pl.when(turn < LINE - 2)
         def _():
@@ -455,14 +450,14 @@
     def _(i):
         turn = LINE - 1 - i
         zz = z_turn(turn)
-        grad_pass([slot(xat(2), zz), slot(xat(1), zz)])
+        grad_pass(2 * zz, [slot(xat(2), zz), slot(xat(1), zz)])
         send_far(turn)
 
         @pl.when(i > 0)
         def _():
             send_near(turn + 1)
 
-        grad_pass([slot(xat(RING - 1), zz), slot(x, zz)])
+        grad_pass(2 * zz + 1, [slot(xat(RING - 1), zz), slot(x, zz)])
 
         @pl.when(i > 1)
         def _():
@@ -472,8 +467,16 @@
         if p == 1:
             send_near(0)
         keys, values, masks, flag = own_tile(p)
-        tiles = [(True, masks[0]), (False, masks[1])]
-        grads = grad_tile(p, keys, values, tiles, 0)
+        scores, dprobs = products(p, keys, values, 0)
+
+        def load(rows):
+            mask = masks[rows.start // HALF]
+            return (
+                jnp.where(mask, scores[rows].reshape(8, 8, COLS) * SCALE2, FAR),
+                dprobs[rows],
+            )
+
+        grads = grad_tile(p, keys.T, [True, False], 0, load)
         rows = own_rows if p == 0 else sib_rows
         for n in range(2):
             lo, hi = grads[n][:HALF, :128], grads[n][HALF:, 128:]
@@ -488,9 +491,9 @@
     for p in range(2):
         unused_small, flag = pair_small(pairs[p])
         turned = flag == 1
+        every = dqacc[p].T * SCALE
         for h in range(GROUP_HEADS):
-            both = dqacc[p, h * HALF : (h + 1) * HALF, :] * SCALE
-            lo, hi = both[:, :128], both[:, 128:]
+            lo, hi = every[h * HALF : (h + 1) * HALF, :128], every[h * HALF : (h + 1) * HALF, 128:]
             dqout[p, :HALF, h * 128 : h * 128 + 128] = jnp.where(turned, hi, lo).astype(BF16)
             dqout[p, HALF:, h * 128 : h * 128 + 128] = jnp.where(turned, lo, hi).astype(BF16)
     dq_out = remote(dqout.at[1], dq_ref.at[:, lanes(core, wide)], brother, DQ)
@@ -564,7 +567,7 @@
             pltpu.VMEM((2, COLS, 256), BF16),
             pltpu.VMEM((3, 2, 2, 8, COLS), F32),
             pltpu.VMEM((2, 2, 8, COLS), jnp.int32),
-            pltpu.VMEM((2, COLS, 256), F32),
+            pltpu.VMEM((2, 256, COLS), F32),
             pltpu.VMEM((slots, 2, 256, 128), F32),
             pltpu.VMEM((128, 128), F32),
             pltpu.VMEM((2, 128, 1024), BF16),
@@ -579,6 +582,7 @@
             pltpu.VMEM(full, BF16),
             pltpu.VMEM(full, BF16),
             pltpu.VMEM(full, BF16),
+            pltpu.VMEM((2 * LINE, 2, 2, 2, 4 * HALF, COLS), F32),
             pltpu.SemaphoreType.DMA((7,)),
             pltpu.SemaphoreType.DMA((COPIES,)),
             pltpu.SemaphoreType.DMA((COPIES,)),

time: 65 us -> 60.5 us (0.931)
  Pallas kernels: 60.1 us -> 56.2 us
    pallas_call x1, Pallas kernels: 60.1 us -> 56.2 us  [per_device(): pl.pallas_call(kernel, out_shape=(jax.ShapeDtypeStruct(q.shape, BF16), ja...]
where the time goes in v4:
time: 60.5 us; the launch traced here: 60.3 us
  Pallas kernels  56.2 us (93%)
  local copies, waits for them, and re-layouts  3.41 us (6%)
  between operations  0.65 us (1%)
    pallas_call x1, Pallas kernels, per_device(): pl.pallas_call(kernel, out_shape=(jax.ShapeDtypeStruct(q.shape, BF16), ja...  56.2 us
    unnamed x7, local copies, waits for them, and re-layouts  3.41 us

profile of v4, /device:TPU:1, one launch (start us, length us, event | category | flops | bytes accessed | tf_op | source)
XLA Modules:
  0.0 60.3 jit_solution(14730296282071903044)
XLA Ops:
  0.6 56.2 %shard_map.85 = (bf16[128,2048]{1,0:T(8,128)(2,1)}, bf16[128,256]{1,0:T(8,128)(2,1)}, bf16[128,256]{1,0:T(8,128)(2,1)}) custom-call(bf16[128,2048]{1,0:T(8,128)(2,1)} %q_ref.1, bf16[128,256]{1,0:T(8,128)(2,1)} %k_ref.1, bf16[128,256]{1,0:T(8,128)(2,1)} %v_ref.1, bf16[128,2048]{1,0:T(8,128)(2,1)} %g_ref.1, s32[16]{0:T(128)} %len_ref.1, s32[64]{0:T(128)} %asg_ref.1), custom_call_target="tpu_custom_call" | custom-call | tf_op jit(solution)/shard_map/pallas_call | solution.py:553
  56.9 0.0 copy-start.1
  56.9 1.9 %copy.12 = bf16[128,2048]{1,0:T(8,128)(2,1)} copy(bf16[128,2048]{1,0:T(8,128)(2,1)} %get-tuple-element.6) | data formatting | bytes 1048576
  58.8 0.0 copy-done.1
  58.8 0.0 copy-start
  58.8 0.6 %copy.13 = bf16[128,256]{1,0:T(8,128)(2,1)} copy(bf16[128,256]{1,0:T(8,128)(2,1)S(1)} %copy-done.1) | data formatting | bytes 131072
  59.4 0.2 copy-done
  59.6 0.6 %copy.14 = bf16[128,256]{1,0:T(8,128)(2,1)} copy(bf16[128,256]{1,0:T(8,128)(2,1)S(1)} %copy-done) | data formatting | bytes 131072
Async XLA Ops:
  56.9 1.9 %copy-start.1 = (bf16[128,256]{1,0:T(8,128)(2,1)S(1)}, bf16[128,256]{1,0:T(8,128)(2,1)}, u32[]{:S(2)}) copy-start(bf16[128,256]{1,0:T(8,128)(2,1)} %get-tuple-element.7) | copy-start | bytes 196612
  58.8 0.9 %copy-start = (bf16[128,256]{1,0:T(8,128)(2,1)S(1)}, bf16[128,256]{1,0:T(8,128)(2,1)}, u32[]{:S(2)}) copy-start(bf16[128,256]{1,0:T(8,128)(2,1)} %get-tuple-element.8) | copy-start | bytes 196612

commit v5 on v4

--- a/solution.py
+++ b/solution.py
@@ -86,20 +86,18 @@
     own_rows, sib_rows = lanes(core, 128), lanes(sib, 128)
     wide = GROUP_HEADS * HEAD_SIZE
     swaps = [
-        remote(k_ref.at[:, lanes(sib, 128)], kv.at[mine, 0, own_rows, :], brother, SWAP),
-        remote(v_ref.at[:, lanes(sib, 128)], kv.at[mine, 1, own_rows, :], brother, SWAP + 1),
+        remote(k_ref.at[:, lanes(sib, 128)], kv.at[mine, core, 0], brother, SWAP),
+        remote(v_ref.at[:, lanes(sib, 128)], kv.at[mine, core, 1], brother, SWAP + 1),
         remote(q_ref.at[:, lanes(sib, wide)], qin.at[1], brother, SWAP + 2),
         remote(g_ref.at[:, lanes(sib, wide)], gin.at[1], brother, SWAP + 3),
     ]
-    for swap in swaps:
-        swap.start()
     own = [
-        pltpu.make_async_copy(k_ref.at[:, lanes(core, 128)], kv.at[mine, 0, own_rows, :], local_sem.at[0]),
-        pltpu.make_async_copy(v_ref.at[:, lanes(core, 128)], kv.at[mine, 1, own_rows, :], local_sem.at[1]),
+        pltpu.make_async_copy(k_ref.at[:, lanes(core, 128)], kv.at[mine, core, 0], local_sem.at[0]),
+        pltpu.make_async_copy(v_ref.at[:, lanes(core, 128)], kv.at[mine, core, 1], local_sem.at[1]),
         pltpu.make_async_copy(q_ref.at[:, lanes(core, wide)], qin.at[0], local_sem.at[2]),
         pltpu.make_async_copy(g_ref.at[:, lanes(core, wide)], gin.at[0], local_sem.at[3]),
     ]
-    for copy in own:
+    for copy in own[:2] + swaps + own[2:]:
         copy.start()
 
     def slot(xx, zz):
@@ -130,38 +128,42 @@
         )
 
     def relay_copies(zz):
-        piece_k = kv.at[slot(xat(RING - 1), zz), 0]
-        piece_v = kv.at[slot(xat(1), zz), 1]
-        return remote(piece_k, piece_k, right, FR + zz), remote(piece_v, piece_v, left, FL + zz)
+        piece_r = kv.at[slot(xat(RING - 1), zz), core]
+        piece_l = kv.at[slot(xat(1), zz), sib]
+        return remote(piece_r, piece_r, right, FR + zz), remote(piece_l, piece_l, left, FL + zz)
 
     def send_piece(zz, n):
         for copy in x_piece(zz, n):
             copy.start()
         z_onward(zz, n, lambda copy: copy.start())
 
+    middle = (z > 0) & (z < LINE - 1)
+
     def z_step(turn):
         zz = z_turn(turn)
-        for n in range(2):
+        for n in (core, sib):
             z_piece(zz, n, up).wait_recv()
             send_piece(zz, n)
 
     def relay(turn):
         zz = z_turn(turn)
         onward = relay_copies(zz)
-        x_piece(zz, 0)[0].wait_recv()
+        x_piece(zz, core)[0].wait_recv()
         onward[0].start()
-        x_piece(zz, 1)[1].wait_recv()
+        x_piece(zz, sib)[1].wait_recv()
         onward[1].start()
 
     def rest_of_x(turn):
         zz = z_turn(turn)
-        x_piece(zz, 0)[1].wait_recv()
-        x_piece(zz, 1)[0].wait_recv()
-
-    for n in range(2):
-        own[n].wait()
-        swaps[n].wait_recv()
-        send_piece(z, n)
+        x_piece(zz, core)[1].wait_recv()
+        x_piece(zz, sib)[0].wait_recv()
+
+    for copy in own[:2]:
+        copy.wait()
+    send_piece(z, core)
+    for swap in swaps[:2]:
+        swap.wait_recv()
+    send_piece(z, sib)
 
     pairs = [2 * chip + core, 2 * chip + sib]
 
@@ -207,10 +209,9 @@
             at = slots[t // 2]
             pair = (lax.rem(at, RING) * LINE + lax.div(at, RING)) * 2 + t % 2
             small, flag = pair_small(pair)
-            row = (t % 2) * 128
             turned = flag == 1
             for n, small_n, large_n in ((0, small_k, large_k), (1, small_v, large_v)):
-                lo, hi = kv[at, n, row : row + HALF, :], kv[at, n, row + HALF : row + 128, :]
+                lo, hi = kv[at, t % 2, n, :HALF, :], kv[at, t % 2, n, HALF:, :]
                 small_n.append(jnp.where(turned, hi, lo))
                 large_n.append(jnp.where(turned, lo, hi))
             firsts.append(small)
@@ -340,13 +341,13 @@
     )
 
     def own_tile(p):
-        rows = own_rows if p == 0 else sib_rows
+        owner = core if p == 0 else sib
         small, flag = pair_small(pairs[p])
         turned = flag == 1
         zero = jnp.zeros((HALF, 128), BF16)
 
         def stack(n):
-            pair = kv[mine, n, rows, :]
+            pair = kv[mine, owner, n]
             lo, hi = pair[:HALF], pair[HALF:]
             return jnp.concatenate(
                 [
@@ -363,9 +364,16 @@
         return stack(0), stack(1), masks, flag
 
     for p in range(2):
-        relay(p)
-        if p == 1:
+        if p == 0:
+            relay(0)
             z_step(2)
+        else:
+
+            @pl.when(middle)
+            def _():
+                z_step(LINE - 1)
+
+            relay(1)
         keys, values, masks, unused_flag = own_tile(p)
         scores, dprobs = products(p, keys, values, 0)
         for side in range(2):
@@ -383,7 +391,7 @@
         zz = z_turn(turn)
         stats_pass(2 * zz + 1, [slot(xat(RING - 1), zz), slot(x, zz)])
 
-        @pl.when(turn == 0)
+        @pl.when((turn == 0) & jnp.logical_not(middle))
         def _():
             z_step(LINE - 1)
 
@@ -560,7 +568,7 @@
         in_specs=[anywhere] * 4 + [smem] * 2,
         out_specs=(anywhere, anywhere, anywhere),
         scratch_shapes=[
-            pltpu.VMEM((slots, 2, 256, 128), BF16),
+            pltpu.VMEM((slots, 2, 2, 128, 128), BF16),
             pltpu.VMEM((2, 128, 1024), BF16),
             pltpu.VMEM((2, 128, 1024), BF16),
             pltpu.VMEM((2, COLS, 256), BF16),

time: 60.5 us -> 59.9 us (0.990)
  the two profiles are of different devices: /device:TPU:1 before, /device:TPU:49 now
where the time goes in v5:
time: 59.9 us; the launch traced here: 59.7 us
  Pallas kernels  55.7 us (93%)
  local copies, waits for them, and re-layouts  3.41 us (6%)
  between operations  0.65 us (1%)
    pallas_call x1, Pallas kernels, per_device(): pl.pallas_call(kernel, out_shape=(jax.ShapeDtypeStruct(q.shape, BF16), ja...  55.7 us
    unnamed x7, local copies, waits for them, and re-layouts  3.41 us

profile of v5, /device:TPU:49, one launch (start us, length us, event | category | flops | bytes accessed | tf_op | source)
XLA Modules:
  0.0 59.7 jit_solution(8290934743545212645)
XLA Ops:
  0.6 55.7 %shard_map.85 = (bf16[128,2048]{1,0:T(8,128)(2,1)}, bf16[128,256]{1,0:T(8,128)(2,1)}, bf16[128,256]{1,0:T(8,128)(2,1)}) custom-call(bf16[128,2048]{1,0:T(8,128)(2,1)} %q_ref.1, bf16[128,256]{1,0:T(8,128)(2,1)} %k_ref.1, bf16[128,256]{1,0:T(8,128)(2,1)} %v_ref.1, bf16[128,2048]{1,0:T(8,128)(2,1)} %g_ref.1, s32[16]{0:T(128)} %len_ref.1, s32[64]{0:T(128)} %asg_ref.1), custom_call_target="tpu_custom_call" | custom-call | tf_op jit(solution)/shard_map/pallas_call | solution.py:561
  56.3 0.0 copy-start.1
  56.3 1.9 %copy.12 = bf16[128,2048]{1,0:T(8,128)(2,1)} copy(bf16[128,2048]{1,0:T(8,128)(2,1)} %get-tuple-element.6) | data formatting | bytes 1048576
  58.2 0.0 copy-done.1
  58.2 0.0 copy-start
  58.2 0.6 %copy.13 = bf16[128,256]{1,0:T(8,128)(2,1)} copy(bf16[128,256]{1,0:T(8,128)(2,1)S(1)} %copy-done.1) | data formatting | bytes 131072
  58.9 0.2 copy-done
  59.1 0.6 %copy.14 = bf16[128,256]{1,0:T(8,128)(2,1)} copy(bf16[128,256]{1,0:T(8,128)(2,1)S(1)} %copy-done) | data formatting | bytes 131072
Async XLA Ops:
  56.3 1.9 %copy-start.1 = (bf16[128,256]{1,0:T(8,128)(2,1)S(1)}, bf16[128,256]{1,0:T(8,128)(2,1)}, u32[]{:S(2)}) copy-start(bf16[128,256]{1,0:T(8,128)(2,1)} %get-tuple-element.7) | copy-start | bytes 196612
  58.2 0.9 %copy-start = (bf16[128,256]{1,0:T(8,128)(2,1)S(1)}, bf16[128,256]{1,0:T(8,128)(2,1)}, u32[]{:S(2)}) copy-start(bf16[128,256]{1,0:T(8,128)(2,1)} %get-tuple-element.8) | copy-start | bytes 196612

commit v6 on v5

--- a/solution.py
+++ b/solution.py
@@ -152,6 +152,16 @@
         onward[0].start()
         x_piece(zz, sib)[1].wait_recv()
         onward[1].start()
+
+    def far_block(zz, target, k):
+        block = kv.at[slot(xat(2), zz)]
+        return remote(block, block, device(x, target, core), FAR_Z + k, FAR_Z)
+
+    def far_sends(do):
+        @pl.when(jnp.logical_not(middle))
+        def _():
+            do(far_block(z, LINE - 1 - z, 0))
+            do(far_block(z, jnp.where(z == 0, 2, 1), 1))
 
     def rest_of_x(turn):
         zz = z_turn(turn)
@@ -385,11 +395,17 @@
             stats[1, p, side] = jnp.sum(probs, axis=0)
             stats[2, p, side] = jnp.sum(probs * dprobs[rows].reshape(8, 8, COLS), axis=0)
 
-    @pl.loop(0, LINE)
+    def far_tile(zz):
+        return 2 * zz, [slot(xat(2), zz), slot(x, zz)]
+
+    def near_tile(zz):
+        return 2 * zz + 1, [slot(xat(RING - 1), zz), slot(xat(1), zz)]
+
+    @pl.loop(0, LINE - 1)
     def _(turn):
         rest_of_x(turn)
         zz = z_turn(turn)
-        stats_pass(2 * zz + 1, [slot(xat(RING - 1), zz), slot(x, zz)])
+        stats_pass(*near_tile(zz))
 
         @pl.when((turn == 0) & jnp.logical_not(middle))
         def _():
@@ -397,11 +413,24 @@
 
         for copy in relay_copies(zz):
             copy.wait_recv()
-        stats_pass(2 * zz, [slot(xat(2), zz), slot(xat(1), zz)])
-
-        @pl.when(turn < LINE - 2)
+
+        @pl.when(turn == 0)
         def _():
-            relay(turn + 2)
+            far_sends(lambda copy: copy.start())
+
+        stats_pass(*far_tile(zz))
+
+        @pl.when(turn == 0)
+        def _():
+            relay(2)
+
+    last = z_turn(LINE - 1)
+    far_block(last, z, 0).wait_recv()
+    stats_pass(*far_tile(last))
+    for n in range(2):
+        for copy in x_piece(last, n):
+            copy.wait_recv()
+    stats_pass(*near_tile(last))
 
     for p in range(2):
         for side in range(2):
@@ -458,22 +487,17 @@
     def _(i):
         turn = LINE - 1 - i
         zz = z_turn(turn)
-        grad_pass(2 * zz, [slot(xat(2), zz), slot(xat(1), zz)])
+        grad_pass(*far_tile(zz))
         send_far(turn)
 
-        @pl.when(i > 0)
-        def _():
-            send_near(turn + 1)
-
-        grad_pass(2 * zz + 1, [slot(xat(RING - 1), zz), slot(x, zz)])
-
-        @pl.when(i > 1)
-        def _():
-            send_last(turn + 2)
+    @pl.loop(0, LINE)
+    def _(i):
+        turn = LINE - 1 - i
+        zz = z_turn(turn)
+        grad_pass(*near_tile(zz))
+        send_near(turn)
 
     for p in range(2):
-        if p == 1:
-            send_near(0)
         keys, values, masks, flag = own_tile(p)
         scores, dprobs = products(p, keys, values, 0)
 
@@ -494,8 +518,6 @@
             )
             part[mine, n, rows, :] += dextra[...]
 
-    send_last(1)
-
     for p in range(2):
         unused_small, flag = pair_small(pairs[p])
         turned = flag == 1
@@ -504,11 +526,13 @@
             lo, hi = every[h * HALF : (h + 1) * HALF, :128], every[h * HALF : (h + 1) * HALF, 128:]
             dqout[p, :HALF, h * 128 : h * 128 + 128] = jnp.where(turned, hi, lo).astype(BF16)
             dqout[p, HALF:, h * 128 : h * 128 + 128] = jnp.where(turned, lo, hi).astype(BF16)
-    dq_out = remote(dqout.at[1], dq_ref.at[:, lanes(core, wide)], brother, DQ)
+    dq_out = remote(dqout.at[1], dq_ref.at[core], brother, DQ)
     dq_out.start()
-    dq_own = pltpu.make_async_copy(dqout.at[0], dq_ref.at[:, lanes(core, wide)], local_sem.at[4])
+    dq_own = pltpu.make_async_copy(dqout.at[0], dq_ref.at[core], local_sem.at[4])
     dq_own.start()
 
+    for turn in (3, 2, 1):
+        send_last(turn)
     part[mine] = x_total(z)
     for k in range(1, LINE):
         there = zat(k)
@@ -519,14 +543,14 @@
             whole = whole + r3[zat(k), n].astype(F32)
         fin[n] = (whole * factor).astype(BF16)
     outs = [
-        remote(fin.at[0, sib_rows, :], dk_ref.at[:, lanes(core, 128)], brother, OUT),
-        remote(fin.at[1, sib_rows, :], dv_ref.at[:, lanes(core, 128)], brother, OUT + 1),
+        remote(fin.at[0, sib_rows, :], dk_ref.at[core], brother, OUT),
+        remote(fin.at[1, sib_rows, :], dv_ref.at[core], brother, OUT + 1),
     ]
     for out in outs:
         out.start()
     keep = [
-        pltpu.make_async_copy(fin.at[0, own_rows, :], dk_ref.at[:, lanes(core, 128)], local_sem.at[5]),
-        pltpu.make_async_copy(fin.at[1, own_rows, :], dv_ref.at[:, lanes(core, 128)], local_sem.at[6]),
+        pltpu.make_async_copy(fin.at[0, own_rows, :], dk_ref.at[core], local_sem.at[5]),
+        pltpu.make_async_copy(fin.at[1, own_rows, :], dv_ref.at[core], local_sem.at[6]),
     ]
     for copy in keep:
         copy.start()
@@ -539,17 +563,25 @@
     for copy in swaps + outs + [dq_out]:
         copy.wait_send()
     for n in range(LINE):
-        for copy in x_piece(n, 0) + x_piece(n, 1) + relay_copies(n) + far_copies(n) + near_copies(n):
+        for copy in x_piece(n, 0) + x_piece(n, 1) + near_copies(n):
             copy.wait_send()
         for piece in range(2):
             z_onward(n, piece, lambda copy: copy.wait_send())
+    for turn in (0, 1, 2):
+        for copy in relay_copies(z_turn(turn)):
+            copy.wait_send()
+    for turn in range(LINE):
+        for copy in far_copies(z_turn(turn)):
+            copy.wait_send()
+    far_sends(lambda copy: copy.wait_send())
     for k in range(1, LINE):
         last_copy(zat(k)).wait_send()
 
 
 SWAP, OUT, DQ, ZED, XR, XL = 0, 4, 6, 8, 24, 32
 FR, FL, C1R, C1L, C2R, C2L, C3 = range(40, 40 + 7 * LINE, LINE)
-COPIES = 40 + 7 * LINE
+FAR_Z = 40 + 7 * LINE
+COPIES = FAR_Z + 2
 
 
 def per_device(q, k, v, g, lengths, assignment):
@@ -558,12 +590,12 @@
     smem = pl.BlockSpec(memory_space=pltpu.SMEM)
     half = (LINE, 256, 128)
     full = (LINE, 2, 256, 128)
-    return pl.pallas_call(
+    halves = pl.pallas_call(
         kernel,
         out_shape=(
-            jax.ShapeDtypeStruct(q.shape, BF16),
-            jax.ShapeDtypeStruct(k.shape, BF16),
-            jax.ShapeDtypeStruct(v.shape, BF16),
+            jax.ShapeDtypeStruct((2, 128, 1024), BF16),
+            jax.ShapeDtypeStruct((2, 128, 128), BF16),
+            jax.ShapeDtypeStruct((2, 128, 128), BF16),
         ),
         in_specs=[anywhere] * 4 + [smem] * 2,
         out_specs=(anywhere, anywhere, anywhere),
@@ -599,6 +631,9 @@
             collective_id=0, has_side_effects=True, vmem_limit_bytes=63 * 1024 * 1024
         ),
     )(q, k, v, g, lengths, assignment)
+    dq, dk, dv = halves
+    dq = dq.transpose(1, 0, 2).reshape(q.shape)
+    return dq, jnp.concatenate([dk[0], dk[1]], axis=1), jnp.concatenate([dv[0], dv[1]], axis=1)
 
 
 def solution(mesh):

time: 59.9 us -> 59.9 us (level)
  the two profiles are of different devices: /device:TPU:49 before, /device:TPU:1 now
where the time goes in v6:
time: 59.9 us; the launch traced here: 59.8 us
  Pallas kernels  55.5 us (93%)
  local copies, waits for them, and re-layouts  2.34 us (4%)
  other arithmetic  1.28 us (2%)
  between operations  0.67 us (1%)
    pallas_call x1, Pallas kernels, per_device(): pl.pallas_call(kernel, out_shape=(jax.ShapeDtypeStruct((2, 128, 1024), BF...  55.5 us
    transpose x1, local copies, waits for them, and re-layouts, per_device(): dq = dq.transpose(1, 0, 2).reshape(q.shape)  1.31 us

profile of v6, /device:TPU:1, one launch (start us, length us, event | category | flops | bytes accessed | tf_op | source)
XLA Modules:
  0.0 59.8 jit_solution(18024478057261990755)
XLA Ops:
  0.6 55.5 %shard_map.85 = (bf16[2,128,1024]{2,1,0:T(8,128)(2,1)}, bf16[2,128,128]{2,1,0:T(8,128)(2,1)}, bf16[2,128,128]{2,1,0:T(8,128)(2,1)}) custom-call(bf16[128,2048]{1,0:T(8,128)(2,1)} %q_ref.1, bf16[128,256]{1,0:T(8,128)(2,1)} %k_ref.1, bf16[128,256]{1,0:T(8,128)(2,1)} %v_ref.1, bf16[128,2048]{1,0:T(8,128)(2,1)} %g_ref.1, s32[16]{0:T(128)} %len_ref.1, s32[64]{0:T(128)} %asg_ref.1), custom_call_target="tpu_custom_call" | custom-call | tf_op jit(solution)/shard_map/pallas_call | solution.py:593
  56.1 1.3 %copy.9 = bf16[128,2,1024]{0,2,1:T(8,128)(2,1)S(1)} copy(bf16[128,2,1024]{2,0,1:T(8,128)(2,1)} %bitcast.11) | data formatting | bytes 1048576 | tf_op jit(solution)/shard_map/transpose | solution.py:635
  57.4 0.0 copy-start
  57.4 0.0 copy-start.1
  57.5 1.0 %copy.10 = bf16[128,2048]{1,0:T(8,128)(2,1)} copy(bf16[128,2048]{0,1:T(8,128)(2,1)S(1)} %bitcast.10) | data formatting | bytes 1048576
  58.5 0.0 copy-done
  58.5 0.0 copy-done.1
  58.5 0.6 %pad_maximum_fusion.1 = bf16[128,256]{1,0:T(8,128)(2,1)} fusion(bf16[128,128]{1,0:T(8,128)(2,1)S(1)} %get-tuple-element.13, bf16[128,128]{1,0:T(8,128)(2,1)S(1)} %get-tuple-element.12), kind=kLoop, calls=%fused_computation.1 | loop fusion | flops 131072 | bytes 131072 | tf_op jit(solution)/shard_map/concatenate | solution.py:636
  59.1 0.6 %pad_maximum_fusion = bf16[128,256]{1,0:T(8,128)(2,1)} fusion(bf16[128,128]{1,0:T(8,128)(2,1)S(1)} %get-tuple-element.16, bf16[128,128]{1,0:T(8,128)(2,1)S(1)} %get-tuple-element.17), kind=kLoop, calls=%fused_computation | loop fusion | flops 131072 | bytes 131072 | tf_op jit(solution)/shard_map/concatenate | solution.py:636
  (1 shorter events, 0.0 us)
Async XLA Ops:
  57.4 1.0 %copy-start = (bf16[2,128,128]{2,1,0:T(8,128)(2,1)S(1)}, bf16[2,128,128]{2,1,0:T(8,128)(2,1)}, u32[]{:S(2)}) copy-start(bf16[2,128,128]{2,1,0:T(8,128)(2,1)} %get-tuple-element.7) | copy-start | bytes 196612
  57.4 1.0 %copy-start.1 = (bf16[2,128,128]{2,1,0:T(8,128)(2,1)S(1)}, bf16[2,128,128]{2,1,0:T(8,128)(2,1)}, u32[]{:S(2)}) copy-start(bf16[2,128,128]{2,1,0:T(8,128)(2,1)} %get-tuple-element.8) | copy-start | bytes 196612

commit v7 on v6

--- a/solution.py
+++ b/solution.py
@@ -133,9 +133,9 @@
         return remote(piece_r, piece_r, right, FR + zz), remote(piece_l, piece_l, left, FL + zz)
 
     def send_piece(zz, n):
+        z_onward(zz, n, lambda copy: copy.start())
         for copy in x_piece(zz, n):
             copy.start()
-        z_onward(zz, n, lambda copy: copy.start())
 
     middle = (z > 0) & (z < LINE - 1)
 
@@ -518,6 +518,8 @@
             )
             part[mine, n, rows, :] += dextra[...]
 
+    send_last(3)
+
     for p in range(2):
         unused_small, flag = pair_small(pairs[p])
         turned = flag == 1
@@ -526,13 +528,13 @@
             lo, hi = every[h * HALF : (h + 1) * HALF, :128], every[h * HALF : (h + 1) * HALF, 128:]
             dqout[p, :HALF, h * 128 : h * 128 + 128] = jnp.where(turned, hi, lo).astype(BF16)
             dqout[p, HALF:, h * 128 : h * 128 + 128] = jnp.where(turned, lo, hi).astype(BF16)
+    send_last(2)
     dq_out = remote(dqout.at[1], dq_ref.at[core], brother, DQ)
     dq_out.start()
     dq_own = pltpu.make_async_copy(dqout.at[0], dq_ref.at[core], local_sem.at[4])
     dq_own.start()
 
-    for turn in (3, 2, 1):
-        send_last(turn)
+    send_last(1)
     part[mine] = x_total(z)
     for k in range(1, LINE):
         there = zat(k)

time: 59.9 us -> 60 us (level)
  no operation moved by 1% of the time
where the time goes in v7:
time: 60 us; the launch traced here: 59.8 us
  Pallas kernels  55.5 us (92%)
  local copies, waits for them, and re-layouts  2.34 us (4%)
  other arithmetic  1.28 us (2%)
  between operations  0.67 us (1%)
    pallas_call x1, Pallas kernels, per_device(): pl.pallas_call(kernel, out_shape=(jax.ShapeDtypeStruct((2, 128, 1024), BF...  55.5 us
    transpose x1, local copies, waits for them, and re-layouts, per_device(): dq = dq.transpose(1, 0, 2).reshape(q.shape)  1.31 us

profile of v7, /device:TPU:1, one launch (start us, length us, event | category | flops | bytes accessed | tf_op | source)
XLA Modules:
  0.0 59.8 jit_solution(8423148570447056211)
XLA Ops:
  0.6 55.5 %shard_map.85 = (bf16[2,128,1024]{2,1,0:T(8,128)(2,1)}, bf16[2,128,128]{2,1,0:T(8,128)(2,1)}, bf16[2,128,128]{2,1,0:T(8,128)(2,1)}) custom-call(bf16[128,2048]{1,0:T(8,128)(2,1)} %q_ref.1, bf16[128,256]{1,0:T(8,128)(2,1)} %k_ref.1, bf16[128,256]{1,0:T(8,128)(2,1)} %v_ref.1, bf16[128,2048]{1,0:T(8,128)(2,1)} %g_ref.1, s32[16]{0:T(128)} %len_ref.1, s32[64]{0:T(128)} %asg_ref.1), custom_call_target="tpu_custom_call" | custom-call | tf_op jit(solution)/shard_map/pallas_call | solution.py:595
  56.2 1.3 %copy.9 = bf16[128,2,1024]{0,2,1:T(8,128)(2,1)S(1)} copy(bf16[128,2,1024]{2,0,1:T(8,128)(2,1)} %bitcast.11) | data formatting | bytes 1048576 | tf_op jit(solution)/shard_map/transpose | solution.py:637
  57.5 0.0 copy-start
  57.5 0.0 copy-start.1
  57.5 1.0 %copy.10 = bf16[128,2048]{1,0:T(8,128)(2,1)} copy(bf16[128,2048]{0,1:T(8,128)(2,1)S(1)} %bitcast.10) | data formatting | bytes 1048576
  58.5 0.0 copy-done
  58.5 0.0 copy-done.1
  58.5 0.6 %pad_maximum_fusion.1 = bf16[128,256]{1,0:T(8,128)(2,1)} fusion(bf16[128,128]{1,0:T(8,128)(2,1)S(1)} %get-tuple-element.13, bf16[128,128]{1,0:T(8,128)(2,1)S(1)} %get-tuple-element.12), kind=kLoop, calls=%fused_computation.1 | loop fusion | flops 131072 | bytes 131072 | tf_op jit(solution)/shard_map/concatenate | solution.py:638
  59.2 0.6 %pad_maximum_fusion = bf16[128,256]{1,0:T(8,128)(2,1)} fusion(bf16[128,128]{1,0:T(8,128)(2,1)S(1)} %get-tuple-element.16, bf16[128,128]{1,0:T(8,128)(2,1)S(1)} %get-tuple-element.17), kind=kLoop, calls=%fused_computation | loop fusion | flops 131072 | bytes 131072 | tf_op jit(solution)/shard_map/concatenate | solution.py:638
  (1 shorter events, 0.0 us)
Async XLA Ops:
  57.5 1.0 %copy-start = (bf16[2,128,128]{2,1,0:T(8,128)(2,1)S(1)}, bf16[2,128,128]{2,1,0:T(8,128)(2,1)}, u32[]{:S(2)}) copy-start(bf16[2,128,128]{2,1,0:T(8,128)(2,1)} %get-tuple-element.7) | copy-start | bytes 196612
  57.5 1.0 %copy-start.1 = (bf16[2,128,128]{2,1,0:T(8,128)(2,1)S(1)}, bf16[2,128,128]{2,1,0:T(8,128)(2,1)}, u32[]{:S(2)}) copy-start(bf16[2,128,128]{2,1,0:T(8,128)(2,1)} %get-tuple-element.8) | copy-start | bytes 196612

commit v8 on v6

--- a/solution.py
+++ b/solution.py
@@ -395,42 +395,40 @@
             stats[1, p, side] = jnp.sum(probs, axis=0)
             stats[2, p, side] = jnp.sum(probs * dprobs[rows].reshape(8, 8, COLS), axis=0)
 
-    def far_tile(zz):
-        return 2 * zz, [slot(xat(2), zz), slot(x, zz)]
-
-    def near_tile(zz):
-        return 2 * zz + 1, [slot(xat(RING - 1), zz), slot(xat(1), zz)]
-
-    @pl.loop(0, LINE - 1)
+    @pl.loop(0, LINE)
     def _(turn):
         rest_of_x(turn)
         zz = z_turn(turn)
-        stats_pass(*near_tile(zz))
+
+        @pl.when(turn == LINE - 1)
+        def _():
+            x_piece(zz, core)[0].wait_recv()
+            x_piece(zz, sib)[1].wait_recv()
+
+        stats_pass(2 * zz + 1, [slot(xat(RING - 1), zz), slot(x, zz)])
 
         @pl.when((turn == 0) & jnp.logical_not(middle))
         def _():
             z_step(LINE - 1)
 
-        for copy in relay_copies(zz):
-            copy.wait_recv()
+        @pl.when(turn < LINE - 1)
+        def _():
+            for copy in relay_copies(zz):
+                copy.wait_recv()
+
+        @pl.when(turn == LINE - 1)
+        def _():
+            far_block(zz, z, 0).wait_recv()
 
         @pl.when(turn == 0)
         def _():
             far_sends(lambda copy: copy.start())
 
-        stats_pass(*far_tile(zz))
+        stats_pass(2 * zz, [slot(xat(2), zz), slot(xat(1), zz)])
 
         @pl.when(turn == 0)
         def _():
             relay(2)
-
-    last = z_turn(LINE - 1)
-    far_block(last, z, 0).wait_recv()
-    stats_pass(*far_tile(last))
-    for n in range(2):
-        for copy in x_piece(last, n):
-            copy.wait_recv()
-    stats_pass(*near_tile(last))
 
     for p in range(2):
         for side in range(2):
@@ -487,14 +485,14 @@
     def _(i):
         turn = LINE - 1 - i
         zz = z_turn(turn)
-        grad_pass(*far_tile(zz))
+        grad_pass(2 * zz, [slot(xat(2), zz), slot(xat(1), zz)])
         send_far(turn)
 
     @pl.loop(0, LINE)
     def _(i):
         turn = LINE - 1 - i
         zz = z_turn(turn)
-        grad_pass(*near_tile(zz))
+        grad_pass(2 * zz + 1, [slot(xat(RING - 1), zz), slot(x, zz)])
         send_near(turn)
 
     for p in range(2):
@@ -631,9 +629,7 @@
             collective_id=0, has_side_effects=True, vmem_limit_bytes=63 * 1024 * 1024
         ),
     )(q, k, v, g, lengths, assignment)
-    dq, dk, dv = halves
-    dq = dq.transpose(1, 0, 2).reshape(q.shape)
-    return dq, jnp.concatenate([dk[0], dk[1]], axis=1), jnp.concatenate([dv[0], dv[1]], axis=1)
+    return tuple(jnp.concatenate([out[0], out[1]], axis=1) for out in halves)
 
 
 def solution(mesh):

time: 59.9 us -> 59.6 us (level)
  local copies, waits for them, and re-layouts: 2.34 us -> 1.1 us
  other arithmetic: 1.28 us -> 2.11 us
    transpose x1 -> x0, local copies, waits for them, and re-layouts: 1.31 us -> none  [per_device(): dq = dq.transpose(1, 0, 2).reshape(q.shape)]
    squeeze x1 -> x2, local copies, waits for them, and re-layouts: 0.01 us -> 1.07 us  [per_device(): return tuple((jnp.concatenate([out[0], out[1]], axis=1) for out in halves))]
    unnamed x5 -> x4, local copies, waits for them, and re-layouts: 1.02 us -> 0.03 us
    concatenate x2 -> x3, other arithmetic: 1.28 us -> 2.11 us  [per_device(): return tuple((jnp.concatenate([out[0], out[1]], axis=1) for out in halves))]
where the time goes in v8:
time: 59.6 us; the launch traced here: 59.5 us
  Pallas kernels  55.6 us (93%)
  other arithmetic  2.11 us (4%)
  local copies, waits for them, and re-layouts  1.1 us (2%)
  between operations  0.66 us (1%)
    pallas_call x1, Pallas kernels, per_device(): pl.pallas_call(kernel, out_shape=(jax.ShapeDtypeStruct((2, 128, 1024), BF...  55.6 us
    concatenate x3, other arithmetic, per_device(): return tuple((jnp.concatenate([out[0], out[1]], axis=1) for out in halves))  2.11 us

profile of v8, /device:TPU:1, one launch (start us, length us, event | category | flops | bytes accessed | tf_op | source)
XLA Modules:
  0.0 59.5 jit_solution(12712692816761658768)
XLA Ops:
  0.6 55.6 %shard_map.85 = (bf16[2,128,1024]{2,1,0:T(8,128)(2,1)}, bf16[2,128,128]{2,1,0:T(8,128)(2,1)}, bf16[2,128,128]{2,1,0:T(8,128)(2,1)}) custom-call(bf16[128,2048]{1,0:T(8,128)(2,1)} %q_ref.1, bf16[128,256]{1,0:T(8,128)(2,1)} %k_ref.1, bf16[128,256]{1,0:T(8,128)(2,1)} %v_ref.1, bf16[128,2048]{1,0:T(8,128)(2,1)} %g_ref.1, s32[16]{0:T(128)} %len_ref.1, s32[64]{0:T(128)} %asg_ref.1), custom_call_target="tpu_custom_call" | custom-call | tf_op jit(solution)/shard_map/pallas_call | solution.py:591
  56.2 1.1 %slice_bitcast_fusion.1 = (bf16[128,1024]{1,0:T(8,128)(2,1)S(1)}, bf16[128,1024]{1,0:T(8,128)(2,1)S(1)}) fusion(bf16[2,128,1024]{2,1,0:T(8,128)(2,1)} %get-tuple-element.6), kind=kLoop, calls=%fused_computation.2 | loop fusion | bytes 1048576 | tf_op jit(solution)/shard_map/squeeze | solution.py:632
  57.3 0.0 copy-start
  57.3 0.0 copy-start.1
  57.3 0.8 %pad_maximum_fusion = bf16[128,2048]{1,0:T(8,128)(2,1)} fusion(bf16[128,1024]{1,0:T(8,128)(2,1)S(1)} %get-tuple-element.10, bf16[128,1024]{1,0:T(8,128)(2,1)S(1)} %get-tuple-element.9), kind=kLoop, calls=%fused_computation | loop fusion | flops 1048576 | bytes 1048576 | tf_op jit(solution)/shard_map/concatenate | solution.py:632
  58.1 0.0 copy-done
  58.2 0.0 copy-done.1
  58.2 0.6 %pad_maximum_fusion.2 = bf16[128,256]{1,0:T(8,128)(2,1)} fusion(bf16[128,128]{1,0:T(8,128)(2,1)S(1)} %get-tuple-element.12, bf16[128,128]{1,0:T(8,128)(2,1)S(1)} %get-tuple-element.11), kind=kLoop, calls=%fused_computation.4 | loop fusion | flops 131072 | bytes 131072 | tf_op jit(solution)/shard_map/concatenate | solution.py:632
  58.8 0.6 %pad_maximum_fusion.1 = bf16[128,256]{1,0:T(8,128)(2,1)} fusion(bf16[128,128]{1,0:T(8,128)(2,1)S(1)} %get-tuple-element.15, bf16[128,128]{1,0:T(8,128)(2,1)S(1)} %get-tuple-element.16), kind=kLoop, calls=%fused_computation.3 | loop fusion | flops 131072 | bytes 131072 | tf_op jit(solution)/shard_map/concatenate | solution.py:632
  (1 shorter events, 0.0 us)
Async XLA Ops:
  57.3 0.9 %copy-start = (bf16[2,128,128]{2,1,0:T(8,128)(2,1)S(1)}, bf16[2,128,128]{2,1,0:T(8,128)(2,1)}, u32[]{:S(2)}) copy-start(bf16[2,128,128]{2,1,0:T(8,128)(2,1)} %get-tuple-element.7) | copy-start | bytes 196612
  57.3 0.9 %copy-start.1 = (bf16[2,128,128]{2,1,0:T(8,128)(2,1)S(1)}, bf16[2,128,128]{2,1,0:T(8,128)(2,1)}, u32[]{:S(2)}) copy-start(bf16[2,128,128]{2,1,0:T(8,128)(2,1)} %get-tuple-element.8) | copy-start | bytes 196612
